TPU v7x, 32 devices: a whole 2x2x4 slice. The times are simulated.
32 devices in a mesh: dp: 8 (over y, x, core), tensor: 4 (over z).
Axes of the slice: x: 2, y: 2, z: 4, core: 2. Of those that a mesh axis runs over, the one named last changes fastest.
Arguments:
- inputs: bfloat16 [3, 8192, 640], P(None, ('dp', 'tensor')), may hold values from -6 to 6
- grad_out: bfloat16 [3, 8192, 640], P(None, ('dp', 'tensor')), may hold values from -6 to 6
- masked: int32 [3, 8192], P(None, 'dp'), may hold values 0 or 1
- bucket: int32 [3, 8], P(None, 'dp'), may hold values from 0 to 2, as said below
- lengths: int32 [3, 32], P(None, 'dp'), may hold values from 1 to 1024, as said below
- first_gain: float32 [640], replicated, may hold values from 0.5 to 1.5
- first_shift: float32 [640], replicated, may hold values from -1.2 to 1.2
- second_gain: float32 [640], replicated, may hold values from 0.5 to 1.5
- second_shift: float32 [640], replicated, may hold values from -1.2 to 1.2
- qkv_weight: bfloat16 [3, 640, 640], P(None, 'dp', 'tensor'), may hold values from -0.25 to 0.25
- qkv_bias: float32 [3, 640], replicated, may hold values from -1.2 to 1.2
- out_weight: bfloat16 [640, 640], P('dp', 'tensor'), may hold values from -2 to 2
- out_bias: float32 [640], replicated, may hold values from -1.2 to 1.2
- up_weight: bfloat16 [640, 2560], P('dp', 'tensor'), may hold values from -0.25 to 0.25
- up_bias: float32 [2560], replicated, may hold values from -1.2 to 1.2
- down_weight: bfloat16 [640, 2560], P('dp', 'tensor'), may hold values from -0.125 to 0.125
- down_bias: float32 [640], replicated, may hold values from -1.2 to 1.2
Outputs:
- layer_out: bfloat16 [3, 8192, 640], P(None, ('dp', 'tensor'))
- grad_inputs: float32 [3, 8192, 640], P(None, ('dp', 'tensor'))
- grad_qkv_weight: float32 [3, 640, 640], P(None, 'dp', 'tensor')
- grad_out_weight: float32 [640, 640], P('dp', 'tensor')
- grad_up_weight: float32 [640, 2560], P('dp', 'tensor')
- grad_down_weight: float32 [640, 2560], P('dp', 'tensor')
- grad_first_gain: float32 [640], replicated
- grad_first_shift: float32 [640], replicated
- grad_second_gain: float32 [640], replicated
- grad_second_shift: float32 [640], replicated
- grad_qkv_bias: float32 [3, 640], replicated
- grad_out_bias: float32 [640], replicated
- grad_up_bias: float32 [2560], replicated
- grad_down_bias: float32 [640], replicated
Inputs may be any that keep to these rules, and one draw needn't show every extreme that they name: Group r of micro-batch m holds sequences in slots of 1024 // 2**bucket[m, r] rows; in every micro-batch one group has 0 and another 2. `lengths`: entry r * 4 + s is the length of the sequence whose slot starts at row s * 256 of group r, where one starts there; other entries are not read. A length is at most its slot's width, and the first sequence of every group fills its slot.
All inputs are finite; a program needn't handle non-finite values. No bound on the sum of `masked` on one device may be relied on, other than what follows from the above.
Results may differ from a plain program's by a relative error of at most 0.015.
Values may be sent and summed in bfloat16 or wider, within the bound.
No kernel may reach another device: no remote copies, remote signals or barrier semaphores. Data moves between devices by JAX's collectives and lax.ppermute only.
A program may use at most 256 MiB of HBM per device.

v0:
```python
import jax
import jax.numpy as jnp
from jax import lax
from jax.sharding import PartitionSpec as P

HEAD_DIM = 32
L_MAX = 1024


def layer_norm(values, gain_row, shift_row):
    average = jnp.mean(values, -1, keepdims=True)
    centred = values - average
    factor = lax.rsqrt(jnp.mean(centred * centred, -1, keepdims=True) + 1e-05)
    unit_rows = centred * factor
    return (unit_rows * gain_row + shift_row, unit_rows, factor)


def norm_back(gradient, unit_rows, factor, gain_row):
    scaled = gradient * gain_row
    return factor * (
        scaled
        - jnp.mean(scaled, -1, keepdims=True)
        - unit_rows * jnp.mean(scaled * unit_rows, -1, keepdims=True)
    )


def layout(bucket_code, slot_lengths, row_total, window):
    quarter = window // 4
    block_rows = jnp.arange(row_total, dtype=jnp.int32)
    seq_width = jnp.int32(window) // jnp.left_shift(jnp.int32(1), bucket_code)
    position = block_rows % seq_width
    sequence = block_rows // seq_width
    slot_index = (block_rows - position) // quarter
    matches = slot_index[:, None] == jnp.arange(slot_lengths.shape[0], dtype=jnp.int32)[None, :]
    length_row = jnp.sum(jnp.where(matches, slot_lengths[None, :], 0), axis=1)
    return (position, sequence, length_row)


def rotary_tables(position, head_dim):
    halfway = head_dim // 2
    frequency = 1.0 / 10000.0 ** (jnp.arange(halfway, dtype=jnp.float32) * 2.0 / head_dim)
    angles = position.astype(jnp.float32)[:, None] * frequency[None, :]
    angles = jnp.concatenate([angles, angles], -1)
    return (jnp.cos(angles)[:, None, :], jnp.sin(angles)[:, None, :])


def rotate(values, cosine, sine_table):
    halfway = values.shape[-1] // 2
    turned = jnp.concatenate([-values[..., halfway:], values[..., :halfway]], -1)
    return values * cosine + turned * sine_table


def rotate_back(gradient, cosine, sine_table):
    halfway = gradient.shape[-1] // 2
    rolled = gradient * sine_table
    return gradient * cosine + jnp.concatenate([rolled[..., halfway:], -rolled[..., :halfway]], -1)


def gelu_slope(values):
    return (
        0.5 * (1.0 + lax.erf(values * 0.7071067811865476))
        + values * jnp.exp(-0.5 * values * values) * 0.3989422804014327
    )


def visibility(sequence, position, length_row, windows, window):
    seq_blocks = sequence.reshape(windows, window)
    pos_blocks = position.reshape(windows, window)
    len_blocks = length_row.reshape(windows, window)
    return (seq_blocks[:, :, None] == seq_blocks[:, None, :]) & (
        pos_blocks[:, None, :] < len_blocks[:, None, :]
    )


def masked_scores(queries, keys_low, visible):
    scores = jnp.einsum("nqhe,nkhe->nhqk", queries, keys_low, preferred_element_type=jnp.float32)
    return jnp.where(visible[:, None], scores, -1e30)


def attend(queries, keys_low, values_low, visible):
    scores = masked_scores(queries, keys_low, visible)
    highest = jnp.max(scores, -1, keepdims=True)
    weights = jnp.exp(scores - highest)
    summed = jnp.sum(weights, -1, keepdims=True)
    probability = (weights / summed).astype(jnp.bfloat16)
    attended = jnp.einsum(
        "nhqk,nkhe->nqhe", probability, values_low, preferred_element_type=jnp.float32
    )
    return (attended, (highest + jnp.log(summed))[..., 0])


def attend_back(queries, keys_low, values_low, visible, log_total, grad_attended):
    scores = masked_scores(queries, keys_low, visible)
    probability = jnp.exp(scores - log_total[..., None])
    prob_low = probability.astype(jnp.bfloat16)
    grad_values = jnp.einsum(
        "nhqk,nqhe->nkhe", prob_low, grad_attended, preferred_element_type=jnp.float32
    )
    grad_prob = jnp.einsum(
        "nqhe,nkhe->nhqk", grad_attended, values_low, preferred_element_type=jnp.float32
    )
    grad_scores = probability * (grad_prob - jnp.sum(probability * grad_prob, -1, keepdims=True))
    grad_scores = grad_scores.astype(jnp.bfloat16)
    grad_queries = jnp.einsum(
        "nhqk,nkhe->nqhe", grad_scores, keys_low, preferred_element_type=jnp.float32
    )
    grad_keys = jnp.einsum(
        "nhqk,nqhe->nkhe", grad_scores, queries, preferred_element_type=jnp.float32
    )
    return (grad_queries, grad_keys, grad_values)


def contract_last(left, right):
    return lax.dot_general(
        left, right, (((1,), (1,)), ((), ())), preferred_element_type=jnp.float32
    )


def contract_first(left, right):
    return lax.dot_general(
        left, right, (((0,), (0,)), ((), ())), preferred_element_type=jnp.float32
    )


def shards(
    inputs,
    grad_out,
    masked,
    bucket,
    lengths,
    first_gain,
    first_shift,
    second_gain,
    second_shift,
    qkv_weight,
    qkv_bias,
    out_weight,
    out_bias,
    up_weight,
    up_bias,
    down_weight,
    down_bias,
):
    tensor_parts = lax.axis_size("tensor")
    tensor_index = lax.axis_index("tensor")
    micro_total = inputs.shape[0]
    rows_local = inputs.shape[1]
    model_width = inputs.shape[2]
    group_rows = rows_local * tensor_parts
    window = min(L_MAX, group_rows)
    windows = group_rows // window
    cols_attn = qkv_weight.shape[2]
    cols_ffn = up_weight.shape[1]
    head_dim = HEAD_DIM
    heads_local = cols_attn // head_dim
    row_start = tensor_index * rows_local
    window_shape = (windows, window, heads_local, head_dim)
    qkv_local_bias = lax.dynamic_slice_in_dim(qkv_bias, tensor_index * cols_attn, cols_attn, 1)
    up_local_bias = lax.dynamic_slice_in_dim(up_bias, tensor_index * cols_ffn, cols_ffn, 0)
    totals = (
        jnp.zeros(qkv_weight.shape, jnp.float32),
        jnp.zeros(out_weight.shape, jnp.float32),
        jnp.zeros(up_weight.shape, jnp.float32),
        jnp.zeros(down_weight.shape, jnp.float32),
    )
    gain_first = jnp.zeros((model_width,), jnp.float32)
    shift_first = jnp.zeros((model_width,), jnp.float32)
    gain_second = jnp.zeros((model_width,), jnp.float32)
    shift_second = jnp.zeros((model_width,), jnp.float32)
    qkv_bias_sum = jnp.zeros((3, cols_attn), jnp.float32)
    out_bias_sum = jnp.zeros((model_width,), jnp.float32)
    up_bias_sum = jnp.zeros((cols_ffn,), jnp.float32)
    down_bias_sum = jnp.zeros((model_width,), jnp.float32)
    outputs = []
    input_grads = []
    for micro_index in range(micro_total):
        current = inputs[micro_index].astype(jnp.float32)
        first_out, first_unit, first_scale = layer_norm(current, first_gain, first_shift)
        first_rows = lax.all_gather(first_out.astype(jnp.bfloat16), "tensor", axis=0, tiled=True)
        attn_full, mix_full, up_full, down_full = (
            lax.all_gather(qkv_weight, "dp", axis=1, tiled=True),
            lax.all_gather(out_weight, "dp", axis=0, tiled=True),
            lax.all_gather(up_weight, "dp", axis=0, tiled=True),
            lax.all_gather(down_weight, "dp", axis=0, tiled=True),
        )
        qkv_rows = (
            jnp.einsum("gd,sdc->sgc", first_rows, attn_full, preferred_element_type=jnp.float32)
            + qkv_local_bias[:, None, :]
        )
        position, sequence, length_row = layout(
            bucket[micro_index, 0], lengths[micro_index], group_rows, window
        )
        cosine, sine_table = rotary_tables(position, head_dim)
        pieces = qkv_rows.reshape(3, group_rows, heads_local, head_dim)
        queries = (
            (rotate(pieces[0], cosine, sine_table) * head_dim ** (-0.5))
            .astype(jnp.bfloat16)
            .reshape(window_shape)
        )
        keys_low = rotate(pieces[1], cosine, sine_table).astype(jnp.bfloat16).reshape(window_shape)
        values_low = pieces[2].astype(jnp.bfloat16).reshape(window_shape)
        visible = visibility(sequence, position, length_row, windows, window)
        attended, log_total = attend(queries, keys_low, values_low, visible)
        attended_low = attended.reshape(group_rows, cols_attn).astype(jnp.bfloat16)
        mixed_rows = lax.psum_scatter(
            contract_last(attended_low, mix_full), "tensor", scatter_dimension=0, tiled=True
        )
        residual = current + mixed_rows + out_bias
        second_out, second_unit, second_scale = layer_norm(residual, second_gain, second_shift)
        second_rows = lax.all_gather(second_out.astype(jnp.bfloat16), "tensor", axis=0, tiled=True)
        up_pre = jnp.dot(second_rows, up_full, preferred_element_type=jnp.float32) + up_local_bias
        hidden = jax.nn.gelu(up_pre, approximate=False).astype(jnp.bfloat16)
        ffn_rows_out = lax.psum_scatter(
            contract_last(hidden, down_full).astype(jnp.bfloat16),
            "tensor",
            scatter_dimension=0,
            tiled=True,
        ).astype(jnp.float32)
        outputs.append((residual + ffn_rows_out + down_bias).astype(jnp.bfloat16))
        counted = jnp.where(position < length_row, masked[micro_index], 0).astype(jnp.float32)
        factor = 3.0 * group_rows / 8.0 / jnp.maximum(jnp.sum(counted), 1.0)
        row_weight = lax.dynamic_slice_in_dim(counted, row_start, rows_local, 0) * factor
        grad_top = grad_out[micro_index].astype(jnp.float32) * row_weight[:, None]
        grad_rows = lax.all_gather(grad_top.astype(jnp.bfloat16), "tensor", axis=0, tiled=True)
        attn_full, mix_full, up_full, down_full = (
            lax.all_gather(qkv_weight, "dp", axis=1, tiled=True),
            lax.all_gather(out_weight, "dp", axis=0, tiled=True),
            lax.all_gather(up_weight, "dp", axis=0, tiled=True),
            lax.all_gather(down_weight, "dp", axis=0, tiled=True),
        )
        grad_down = contract_first(grad_rows, hidden)
        grad_hidden = jnp.dot(grad_rows, down_full, preferred_element_type=jnp.float32)
        grad_up_pre = (grad_hidden * gelu_slope(up_pre)).astype(jnp.bfloat16)
        grad_up = contract_first(second_rows, grad_up_pre)
        grad_second = lax.psum_scatter(
            contract_last(grad_up_pre, up_full), "tensor", scatter_dimension=0, tiled=True
        )
        grad_residual = grad_top + norm_back(grad_second, second_unit, second_scale, second_gain)
        grad_mix_rows = lax.all_gather(
            grad_residual.astype(jnp.bfloat16), "tensor", axis=0, tiled=True
        )
        grad_mix = contract_first(grad_mix_rows, attended_low)
        grad_attended = jnp.dot(grad_mix_rows, mix_full, preferred_element_type=jnp.float32).astype(
            jnp.bfloat16
        )
        grad_queries, grad_keys, grad_values = attend_back(
            queries, keys_low, values_low, visible, log_total, grad_attended.reshape(window_shape)
        )
        grad_queries = rotate_back(
            grad_queries.reshape(group_rows, heads_local, head_dim), cosine, sine_table
        ) * head_dim ** (-0.5)
        grad_keys = rotate_back(
            grad_keys.reshape(group_rows, heads_local, head_dim), cosine, sine_table
        )
        grad_qkv = jnp.stack(
            [
                grad_queries.reshape(group_rows, cols_attn),
                grad_keys.reshape(group_rows, cols_attn),
                grad_values.reshape(group_rows, cols_attn),
            ]
        ).astype(jnp.bfloat16)
        grad_attn = jnp.einsum(
            "gd,sgc->sdc", first_rows, grad_qkv, preferred_element_type=jnp.float32
        )
        grad_first = lax.psum_scatter(
            jnp.einsum(
                "sgc,sdc->gd", grad_qkv, attn_full, preferred_element_type=jnp.float32
            ).astype(jnp.bfloat16),
            "tensor",
            scatter_dimension=0,
            tiled=True,
        ).astype(jnp.float32)
        input_grads.append(
            grad_residual + norm_back(grad_first, first_unit, first_scale, first_gain)
        )
        gain_first = gain_first + jnp.sum(grad_first * first_unit, 0)
        shift_first = shift_first + jnp.sum(grad_first, 0)
        gain_second = gain_second + jnp.sum(grad_second * second_unit, 0)
        shift_second = shift_second + jnp.sum(grad_second, 0)
        qkv_bias_sum = qkv_bias_sum + jnp.sum(grad_qkv.astype(jnp.float32), 1)
        out_bias_sum = out_bias_sum + jnp.sum(grad_residual, 0)
        up_bias_sum = up_bias_sum + jnp.sum(grad_up_pre.astype(jnp.float32), 0)
        down_bias_sum = down_bias_sum + jnp.sum(grad_top, 0)
        shard_attn, shard_mix, shard_up, shard_down = (
            lax.psum_scatter(grad_attn, "dp", scatter_dimension=1, tiled=True),
            lax.psum_scatter(grad_mix, "dp", scatter_dimension=0, tiled=True),
            lax.psum_scatter(grad_up, "dp", scatter_dimension=0, tiled=True),
            lax.psum_scatter(grad_down, "dp", scatter_dimension=0, tiled=True),
        )
        totals = (
            totals[0] + shard_attn,
            totals[1] + shard_mix,
            totals[2] + shard_up,
            totals[3] + shard_down,
        )
    qkv_bias_full = lax.dynamic_update_slice_in_dim(
        jnp.zeros((3, model_width), jnp.float32), qkv_bias_sum, tensor_index * cols_attn, 1
    )
    up_bias_full = lax.dynamic_update_slice_in_dim(
        jnp.zeros((up_bias.shape[0],), jnp.float32), up_bias_sum, tensor_index * cols_ffn, 0
    )
    small_sums = lax.psum(
        (
            gain_first,
            shift_first,
            gain_second,
            shift_second,
            qkv_bias_full,
            out_bias_sum,
            up_bias_full,
            down_bias_sum,
        ),
        ("dp", "tensor"),
    )
    return (
        jnp.stack(outputs),
        jnp.stack(input_grads),
        totals[0],
        totals[1],
        totals[2],
        totals[3],
        small_sums[0],
        small_sums[1],
        small_sums[2],
        small_sums[3],
        small_sums[4],
        small_sums[5],
        small_sums[6],
        small_sums[7],
    )


def solution(mesh):
    placed = (
        P(None, ("dp", "tensor"), None),
        P(None, ("dp", "tensor"), None),
        P(None, "dp"),
        P(None, "dp"),
        P(None, "dp"),
        P(),
        P(),
        P(),
        P(),
        P(None, "dp", "tensor"),
        P(),
        P("dp", "tensor"),
        P(),
        P("dp", "tensor"),
        P(),
        P("dp", "tensor"),
        P(),
    )
    return jax.shard_map(
        shards,
        mesh=mesh,
        in_specs=placed,
        out_specs=(
            P(None, ("dp", "tensor"), None),
            P(None, ("dp", "tensor"), None),
            P(None, "dp", "tensor"),
            P("dp", "tensor"),
            P("dp", "tensor"),
            P("dp", "tensor"),
            P(),
            P(),
            P(),
            P(),
            P(),
            P(),
            P(),
            P(),
        ),
        check_vma=False,
    )
```

profile of v0, /device:TPU:0, one launch (start us, length us, event | category | flops | bytes accessed | tf_op | source)
XLA Modules:
  0.0 1237.4 jit_solution(9624351047308675038)
XLA Ops:
  19.8 13.7 %all_gather.33 = bf16[3,640,160]{2,0,1:T(4,128)(2,1)S(1)} all-gather(bf16[3,80,160]{2,0,1:T(4,128)(2,1)S(1)} %copy.68), channel_id=1, replica_groups=mesh['dp'=8,'tensor'=4] {'dp'}, dimensions={1}, use_global_device_ids=true | all-gather | bytes 691200 | tf_op jit(solution)/shard_map/all_gather | solution.py:181
  37.3 8.8 all_gather.34
  55.7 26.3 %all-gather.17.cloned.1.call-done = bf16[1024,640]{1,0:T(8,128)(2,1)} async-done(((bf16[256,640]{1,0:T(8,128)(2,1)}), bf16[1024,640]{1,0:T(8,128)(2,1)}) %all-gather.17.cloned.1.call-update) | async-done | bytes 1310736 | tf_op jit(solution)/shard_map/all_gather | solution.py:179
  85.7 30.2 %all-gather.13.cloned.1.call-done = bf16[1024,640]{1,0:T(8,128)(2,1)} async-done(((bf16[256,640]{1,0:T(8,128)(2,1)}), bf16[1024,640]{1,0:T(8,128)(2,1)}) %all-gather.13.cloned.1.call-update) | async-done | bytes 1310736 | tf_op jit(solution)/shard_map/all_gather | solution.py:179
  136.2 5.3 fusion.82
  157.5 5.3 fusion.81
  177.8 5.3 fusion.80
  185.4 10.2 reduce-scatter.19.cloned.1.call-done
  195.7 54.0 %reduce-scatter.23.cloned.1.call-done = f32[256,640]{1,0:T(8,128)} async-done(((f32[1024,640]{1,0:T(8,128)}), f32[256,640]{1,0:T(8,128)}) %reduce-scatter.23.cloned.1.call-update) | async-done | bytes 655376 | tf_op jit(solution)/shard_map/reduce_scatter | solution.py:205
  249.7 54.0 %reduce-scatter.27.cloned.1.call-done = f32[256,640]{1,0:T(8,128)} async-done(((f32[1024,640]{1,0:T(8,128)}), f32[256,640]{1,0:T(8,128)}) %reduce-scatter.27.cloned.1.call-update) | async-done | bytes 655376 | tf_op jit(solution)/shard_map/reduce_scatter | solution.py:205
  312.3 10.5 all_gather.72
  322.8 11.6 all_gather.73
  334.4 5.8 all-gather.19.cloned.1.call-done
  344.4 29.1 %all-gather.29.cloned.1.call-done = bf16[1024,640]{1,0:T(8,128)(2,1)} async-done(((bf16[256,640]{1,0:T(8,128)(2,1)}), bf16[1024,640]{1,0:T(8,128)(2,1)}) %all-gather.29.cloned.1.call-update) | async-done | bytes 1310736 | tf_op jit(solution)/shard_map/all_gather | solution.py:224
  373.5 4.8 convert_reduce_fusion.1
  382.3 24.5 %all-gather.23.cloned.1.call-done = bf16[1024,640]{1,0:T(8,128)(2,1)} async-done(((bf16[256,640]{1,0:T(8,128)(2,1)}), bf16[1024,640]{1,0:T(8,128)(2,1)}) %all-gather.23.cloned.1.call-update) | async-done | bytes 1310736 | tf_op jit(solution)/shard_map/all_gather | solution.py:210
  410.9 29.6 %all-gather.15.cloned.1.call-done = bf16[1024,640]{1,0:T(8,128)(2,1)} async-done(((bf16[256,640]{1,0:T(8,128)(2,1)}), bf16[1024,640]{1,0:T(8,128)(2,1)}) %all-gather.15.cloned.1.call-update) | async-done | bytes 1310736 | tf_op jit(solution)/shard_map/all_gather | solution.py:210
  440.6 19.5 %fusion.20 = (bf16[1024,640]{1,0:T(8,128)(2,1)}, bf16[1024,640]{1,0:T(8,128)(2,1)S(1)}, bf16[1024,640]{1,0:T(8,128)(2,1)}, f32[1024,640]{1,0:T(8,128)}) fusion(f32[640]{0:T(1024)S(1)} %dynamic_slice.16, f32[1024,640]{1,0:T(8,128)} %fusion.260, f32[1024,640]{1,0:T(8,128)} %fusion.263, bf16[1024,640]{1,0:T(8,128)(2,1)} %all-gather.15.cloned.1.call-done, ...), kind=kOutput, calls=%fused_computation.44 | convolution fusion | flops 968622080 | bytes 13928960 | tf_op jit(solution)/shard_map/dot_general | solution.py:211
  466.7 27.3 %reduce-scatter.35.cloned.1.call-done = f32[256,640]{1,0:T(8,128)} async-done(((f32[1024,640]{1,0:T(8,128)}), f32[256,640]{1,0:T(8,128)}) %reduce-scatter.35.cloned.1.call-update) | async-done | bytes 655376 | tf_op jit(solution)/shard_map/reduce_scatter | solution.py:235
  496.1 31.0 %reduce-scatter.25.cloned.1.call-done = bf16[256,640]{1,0:T(8,128)(2,1)} async-done(((bf16[1024,640]{1,0:T(8,128)(2,1)}), bf16[256,640]{1,0:T(8,128)(2,1)}) %reduce-scatter.25.cloned.1.call-update) | async-done | bytes 327696 | tf_op jit(solution)/shard_map/reduce_scatter | solution.py:213
  538.7 23.4 %all-gather.33.cloned.1.call-done = bf16[1024,640]{1,0:T(8,128)(2,1)} async-done(((bf16[256,640]{1,0:T(8,128)(2,1)}), bf16[1024,640]{1,0:T(8,128)(2,1)}) %all-gather.33.cloned.1.call-update) | async-done | bytes 1310736 | tf_op jit(solution)/shard_map/all_gather | solution.py:224
  562.1 4.5 convert_reduce_fusion
  570.7 24.5 %all-gather.25.cloned.1.call-done = bf16[1024,640]{1,0:T(8,128)(2,1)} async-done(((bf16[256,640]{1,0:T(8,128)(2,1)}), bf16[1024,640]{1,0:T(8,128)(2,1)}) %all-gather.25.cloned.1.call-update) | async-done | bytes 1310736 | tf_op jit(solution)/shard_map/all_gather | solution.py:224
  604.2 24.2 %all-gather.31.cloned.1.call-done = bf16[1024,640]{1,0:T(8,128)(2,1)} async-done(((bf16[256,640]{1,0:T(8,128)(2,1)}), bf16[1024,640]{1,0:T(8,128)(2,1)}) %all-gather.31.cloned.1.call-update) | async-done | bytes 1310736 | tf_op jit(solution)/shard_map/all_gather | solution.py:239
  630.4 14.5 %multiply_reduce_fusion.1 = (f32[5,1024]{1,0:T(8,128)S(1)}, f32[5,1024,1024]{1,2,0:T(8,128)}) fusion(f32[5,1024,1024]{1,2,0:T(8,128)} %copy-done.4, f32[5,1024]{1,0:T(8,128)S(1)} %log_add_fusion.1, pred[1024,1024]{0,1:T(8,128)(4,1)S(1)} %copy-done.11, bf16[1024,5,32]{0,2,1:T(8,128)(2,1)S(1)} %bitcast.462, bf16[1024,5,32]{0,2,1:T(8,128)(2,1)S(1)} %bitcast.461), kind=kOutput, calls=%fused_computation.4 | convolution fusion | flops 356510720 | bytes 43687936 | tf_op jit(solution)/shard_map/nqhe,nkhe->nhqk/dot_general | solution.py:99
  644.9 15.3 %multiply_convert_fusion.1 = bf16[5,1024,1024]{1,2,0:T(8,128)(2,1)S(1)} fusion(f32[5,1024,1024]{1,2,0:T(8,128)} %get-tuple-element.231, f32[5,1024,1024]{1,2,0:T(8,128)} %copy-done.4, f32[5,1024]{1,0:T(8,128)S(1)} %get-tuple-element.230, f32[5,1024]{1,0:T(8,128)S(1)} %log_add_fusion.1, pred[1024,1024]{0,1:T(8,128)(4,1)S(1)} %copy-done.11), kind=kLoop, calls=%fused_computation.3 | loop fusion | flops 26214400 | bytes 53518336 | tf_op jit(solution)/shard_map/convert_element_type | solution.py:103
  666.7 26.3 %reduce-scatter.29.cloned.1.call-done = bf16[256,640]{1,0:T(8,128)(2,1)} async-done(((bf16[1024,640]{1,0:T(8,128)(2,1)}), bf16[256,640]{1,0:T(8,128)(2,1)}) %reduce-scatter.29.cloned.1.call-update) | async-done | bytes 327696 | tf_op jit(solution)/shard_map/reduce_scatter | solution.py:213
  693.0 53.1 %reduce-scatter.39.cloned.1.call-done = f32[256,640]{1,0:T(8,128)} async-done(((f32[1024,640]{1,0:T(8,128)}), f32[256,640]{1,0:T(8,128)}) %reduce-scatter.39.cloned.1.call-update) | async-done | bytes 655376 | tf_op jit(solution)/shard_map/reduce_scatter | solution.py:235
  746.1 54.1 %reduce-scatter.31.cloned.1.call-done = f32[256,640]{1,0:T(8,128)} async-done(((f32[1024,640]{1,0:T(8,128)}), f32[256,640]{1,0:T(8,128)}) %reduce-scatter.31.cloned.1.call-update) | async-done | bytes 655376 | tf_op jit(solution)/shard_map/reduce_scatter | solution.py:235
  810.4 10.5 fusion.74
  821.8 18.4 %all-gather.35.cloned.1.call-done = bf16[1024,640]{1,0:T(8,128)(2,1)} async-done(((bf16[256,640]{1,0:T(8,128)(2,1)}), bf16[1024,640]{1,0:T(8,128)(2,1)}) %all-gather.35.cloned.1.call-update) | async-done | bytes 1310736 | tf_op jit(solution)/shard_map/all_gather | solution.py:239
  842.2 10.3 fusion.77
  852.5 14.5 %multiply_reduce_fusion = (f32[5,1024]{1,0:T(8,128)S(1)}, f32[5,1024,1024]{1,2,0:T(8,128)}) fusion(f32[5,1024,1024]{1,2,0:T(8,128)} %copy-done.3, f32[5,1024]{1,0:T(8,128)S(1)} %log_add_fusion, pred[1024,1024]{0,1:T(8,128)(4,1)S(1)} %copy-done.9, bf16[1024,5,32]{0,2,1:T(8,128)(2,1)S(1)} %bitcast.467, bf16[1024,5,32]{0,2,1:T(8,128)(2,1)S(1)} %bitcast.459), kind=kOutput, calls=%fused_computation.1 | convolution fusion | flops 356510720 | bytes 43687936 | tf_op jit(solution)/shard_map/nqhe,nkhe->nhqk/dot_general | solution.py:99
  867.0 6.5 all-gather.27.cloned.1.call-done
  875.5 10.1 fusion.71
  885.6 14.4 %multiply_reduce_fusion.2 = (f32[5,1024]{1,0:T(8,128)S(1)}, f32[5,1024,1024]{1,2,0:T(8,128)}) fusion(f32[5,1024,1024]{1,2,0:T(8,128)} %copy-done.2, f32[5,1024]{1,0:T(8,128)S(1)} %log_add_fusion.2, pred[1024,1024]{0,1:T(8,128)(4,1)S(1)} %copy-done.7, bf16[1024,5,32]{0,2,1:T(8,128)(2,1)S(1)} %bitcast.465, bf16[1024,5,32]{0,2,1:T(8,128)(2,1)S(1)} %bitcast.457), kind=kOutput, calls=%fused_computation.7 | convolution fusion | flops 356510720 | bytes 43687936 | tf_op jit(solution)/shard_map/nqhe,nkhe->nhqk/dot_general | solution.py:99
  900.1 21.7 %multiply_convert_fusion = bf16[5,1024,1024]{1,2,0:T(8,128)(2,1)} fusion(f32[5,1024,1024]{1,2,0:T(8,128)} %get-tuple-element.228, f32[5,1024,1024]{1,2,0:T(8,128)} %copy-done.3, f32[5,1024]{1,0:T(8,128)S(1)} %get-tuple-element.227, f32[5,1024]{1,0:T(8,128)S(1)} %log_add_fusion, pred[1024,1024]{0,1:T(8,128)(4,1)S(1)} %copy-done.9), kind=kLoop, calls=%fused_computation | loop fusion | flops 26214400 | bytes 53518336 | tf_op jit(solution)/shard_map/convert_element_type | solution.py:103
  921.8 7.2 fusion.269
  929.0 6.1 bitcast_multiply_fusion.7
  935.3 14.9 %multiply_convert_fusion.2 = bf16[5,1024,1024]{1,2,0:T(8,128)(2,1)} fusion(f32[5,1024,1024]{1,2,0:T(8,128)} %get-tuple-element.234, f32[5,1024,1024]{1,2,0:T(8,128)S(1)} %bitcast.439, f32[5,1024]{1,0:T(8,128)S(1)} %get-tuple-element.233, f32[5,1024]{1,0:T(8,128)S(1)} %log_add_fusion.2, pred[1024,1024]{0,1:T(8,128)(4,1)S(1)} %copy-done.7), kind=kLoop, calls=%fused_computation.6 | loop fusion | flops 26214400 | bytes 53518336 | tf_op jit(solution)/shard_map/convert_element_type | solution.py:103
  950.2 7.3 fusion.265
  1003.1 6.5 reduce-scatter.49.cloned.1.call-done
  1011.5 31.7 %reduce-scatter.37.cloned.1.call-done = bf16[256,640]{1,0:T(8,128)(2,1)} async-done(((bf16[1024,640]{1,0:T(8,128)(2,1)}), bf16[256,640]{1,0:T(8,128)(2,1)}) %reduce-scatter.37.cloned.1.call-update) | async-done | bytes 327696 | tf_op jit(solution)/shard_map/reduce_scatter | solution.py:265
  1043.2 32.2 %reduce-scatter.41.cloned.1.call-done = bf16[256,640]{1,0:T(8,128)(2,1)} async-done(((bf16[1024,640]{1,0:T(8,128)(2,1)}), bf16[256,640]{1,0:T(8,128)(2,1)}) %reduce-scatter.41.cloned.1.call-update) | async-done | bytes 327696 | tf_op jit(solution)/shard_map/reduce_scatter | solution.py:265
  1075.4 32.3 %reduce-scatter.33.cloned.1.call-done = bf16[256,640]{1,0:T(8,128)(2,1)} async-done(((bf16[1024,640]{1,0:T(8,128)(2,1)}), bf16[256,640]{1,0:T(8,128)(2,1)}) %reduce-scatter.33.cloned.1.call-update) | async-done | bytes 327696 | tf_op jit(solution)/shard_map/reduce_scatter | solution.py:265
  1110.1 40.6 %all-reduce = (f32[640]{0:T(1024)}, f32[640]{0:T(1024)}, f32[640]{0:T(1024)}, f32[640]{0:T(1024)}, f32[3,640]{1,0:T(4,128)}, /*index=5*/f32[640]{0:T(1024)}, f32[2560]{0:T(1024)}, f32[640]{0:T(1024)}) all-reduce(f32[640]{0:T(1024)S(1)} %add_add_fusion.8, ...), channel_id=1, replica_groups=mesh['dp'=8,'tensor'=4] {'dp','tensor'}, use_global_device_ids=true, to_apply=%region_66.67 | all-reduce | flops 8320 | bytes 66560 | tf_op jit(solution)/shard_map/psum | solution.py:302
  1154.9 37.2 %reduce-scatter.47.cloned.1.call-done = f32[80,640]{1,0:T(8,128)} async-done(((f32[640,640]{1,0:T(8,128)}), f32[80,640]{1,0:T(8,128)}) %reduce-scatter.47.cloned.1.call-update) | async-done | bytes 204816 | tf_op jit(solution)/shard_map/reduce_scatter | solution.py:288
  1192.1 38.3 %reduce-scatter.43.cloned.1.call-done = f32[80,160]{1,0:T(8,128)} async-done(((f32[640,160]{1,0:T(8,128)}), f32[80,160]{1,0:T(8,128)}) %reduce-scatter.43.cloned.1.call-update) | async-done | bytes 51216 | tf_op jit(solution)/shard_map/reduce_scatter | solution.py:286
  (598 shorter events, 208.5 us)
Async XLA Ops:
  7.2 44.4 %all-gather.21.cloned.1.call-start = ((), (), s32[]{:S(2)}) async-start(), calls=%async_computation.24 | async-start | bytes 1638400 | tf_op jit(solution)/shard_map/all_gather | solution.py:179
  12.6 69.4 %all-gather.17.cloned.1.call-start = ((), (), s32[]{:S(2)}) async-start(), calls=%async_computation.20 | async-start | bytes 1638400 | tf_op jit(solution)/shard_map/all_gather | solution.py:179
  13.3 102.5 %all-gather.13.cloned.1.call-start = ((), (), s32[]{:S(2)}) async-start(), calls=%async_computation.16 | async-start | bytes 1638400 | tf_op jit(solution)/shard_map/all_gather | solution.py:179
  14.1 181.6 %reduce-scatter.19.cloned.1.call-start = ((), (), s32[]{:S(2)}) async-start(), calls=%async_computation.17 | async-start | bytes 3276800 | tf_op jit(solution)/shard_map/reduce_scatter | solution.py:205
  49.5 125.2 %copy-start.8 = (pred[1024,1024]{0,1:T(8,128)(4,1)}, pred[1024,1024]{0,1:T(8,128)(4,1)S(1)}, u32[]{:S(2)}) copy-start(pred[1024,1024]{0,1:T(8,128)(4,1)S(1)} %compare_and_fusion) | copy-start | bytes 3145732
  144.4 105.2 %reduce-scatter.23.cloned.1.call-start = ((), (), s32[]{:S(2)}) async-start(), calls=%async_computation.21 | async-start | bytes 3276800 | tf_op jit(solution)/shard_map/reduce_scatter | solution.py:205
  165.1 138.6 %reduce-scatter.27.cloned.1.call-start = ((), (), s32[]{:S(2)}) async-start(), calls=%async_computation.25 | async-start | bytes 3276800 | tf_op jit(solution)/shard_map/reduce_scatter | solution.py:205
  183.1 120.5 %copy-start.13 = (bf16[3,256,640]{2,1,0:T(8,128)(2,1)S(1)}, bf16[3,256,640]{2,1,0:T(8,128)(2,1)}, u32[]{:S(2)}) copy-start(bf16[3,256,640]{2,1,0:T(8,128)(2,1)} %param.17) | copy-start | bytes 2949124
  183.1 120.5 %copy-start.167 = (f32[640]{0:T(1024)S(1)}, f32[640]{0:T(1024)}, u32[]{:S(2)}) copy-start(f32[640]{0:T(1024)} %param.29) | copy-start | bytes 7684
  185.4 121.0 %copy-start.122 = (f32[640]{0:T(1024)S(1)}, f32[640]{0:T(1024)}, u32[]{:S(2)}) copy-start(f32[640]{0:T(1024)} %param.24) | copy-start | bytes 7684
  185.4 120.9 %copy-start.163 = (f32[640]{0:T(1024)S(1)}, f32[640]{0:T(1024)}, u32[]{:S(2)}) copy-start(f32[640]{0:T(1024)} %param.25) | copy-start | bytes 7684
  185.4 154.9 %all-gather.19.cloned.1.call-start = ((), (), s32[]{:S(2)}) async-start(), calls=%async_computation.22 | async-start | bytes 1638400 | tf_op jit(solution)/shard_map/all_gather | solution.py:210
  307.7 65.8 %all-gather.29.cloned.1.call-start = ((), (), s32[]{:S(2)}) async-start(), calls=%async_computation.32 | async-start | bytes 1638400 | tf_op jit(solution)/shard_map/all_gather | solution.py:224
  310.1 96.7 %all-gather.23.cloned.1.call-start = ((), (), s32[]{:S(2)}) async-start(), calls=%async_computation.26 | async-start | bytes 1638400 | tf_op jit(solution)/shard_map/all_gather | solution.py:210
  310.9 129.7 %all-gather.15.cloned.1.call-start = ((), (), s32[]{:S(2)}) async-start(), calls=%async_computation.18 | async-start | bytes 1638400 | tf_op jit(solution)/shard_map/all_gather | solution.py:210
  311.5 182.5 %reduce-scatter.35.cloned.1.call-start = ((), (), s32[]{:S(2)}) async-start(), calls=%async_computation.33 | async-start | bytes 3276800 | tf_op jit(solution)/shard_map/reduce_scatter | solution.py:235
  322.8 117.8 %copy-start.97 = (bf16[640,640]{1,0:T(8,128)(2,1)}, bf16[640,640]{1,0:T(8,128)(2,1)S(1)}, u32[]{:S(2)}) copy-start(bf16[640,640]{1,0:T(8,128)(2,1)S(1)} %all_gather.72) | copy-start | bytes 2457604
  382.3 144.8 %reduce-scatter.25.cloned.1.call-start = ((), (), s32[]{:S(2)}) async-start(), calls=%async_computation.23 | async-start | bytes 1638400 | tf_op jit(solution)/shard_map/reduce_scatter | solution.py:213
  463.6 98.5 %all-gather.33.cloned.1.call-start = ((), (), s32[]{:S(2)}) async-start(), calls=%async_computation.36 | async-start | bytes 1638400 | tf_op jit(solution)/shard_map/all_gather | solution.py:224
  530.5 64.8 %all-gather.25.cloned.1.call-start = ((), (), s32[]{:S(2)}) async-start(), calls=%async_computation.28 | async-start | bytes 1638400 | tf_op jit(solution)/shard_map/all_gather | solution.py:224
  531.0 97.4 %all-gather.31.cloned.1.call-start = ((), (), s32[]{:S(2)}) async-start(), calls=%async_computation.34 | async-start | bytes 1638400 | tf_op jit(solution)/shard_map/all_gather | solution.py:239
  531.9 134.8 %reduce-scatter.21.cloned.1.call-start = ((), (), s32[]{:S(2)}) async-start(), calls=%async_computation.19 | async-start | bytes 1638400 | tf_op jit(solution)/shard_map/reduce_scatter | solution.py:213
  536.1 156.9 %reduce-scatter.29.cloned.1.call-start = ((), (), s32[]{:S(2)}) async-start(), calls=%async_computation.27 | async-start | bytes 1638400 | tf_op jit(solution)/shard_map/reduce_scatter | solution.py:213
  538.7 207.4 %reduce-scatter.39.cloned.1.call-start = ((), (), s32[]{:S(2)}) async-start(), calls=%async_computation.37 | async-start | bytes 3276800 | tf_op jit(solution)/shard_map/reduce_scatter | solution.py:235
  570.6 229.6 %reduce-scatter.31.cloned.1.call-start = ((), (), s32[]{:S(2)}) async-start(), calls=%async_computation.29 | async-start | bytes 3276800 | tf_op jit(solution)/shard_map/reduce_scatter | solution.py:235
  603.8 236.5 %all-gather.35.cloned.1.call-start = ((), (), s32[]{:S(2)}) async-start(), calls=%async_computation.38 | async-start | bytes 1638400 | tf_op jit(solution)/shard_map/all_gather | solution.py:239
  663.4 136.8 %copy-start.16 = (f32[256,640]{1,0:T(8,128)S(1)}, f32[256,640]{1,0:T(8,128)}, u32[]{:S(2)}) copy-start(f32[256,640]{1,0:T(8,128)} %copy-done.15) | copy-start | bytes 1966084
  663.4 136.8 %copy-start.18 = (f32[256,640]{1,0:T(8,128)S(1)}, f32[256,640]{1,0:T(8,128)}, u32[]{:S(2)}) copy-start(f32[256,640]{1,0:T(8,128)} %copy-done.17) | copy-start | bytes 1966084
  663.4 136.8 %copy-start.132 = (f32[256]{0:T(256)S(1)}, f32[256]{0:T(256)}, u32[]{:S(2)}) copy-start(f32[256]{0:T(256)} %copy-done.131) | copy-start | bytes 3076
  663.4 136.8 %copy-start.134 = (f32[256]{0:T(256)S(1)}, f32[256]{0:T(256)}, u32[]{:S(2)}) copy-start(f32[256]{0:T(256)} %copy-done.133) | copy-start | bytes 3076
  666.6 137.3 %copy-start.150 = (f32[256]{0:T(256)S(1)}, f32[256]{0:T(256)}, u32[]{:S(2)}) copy-start(f32[256]{0:T(256)} %copy-done.149) | copy-start | bytes 3076
  666.6 137.3 %copy-start.152 = (f32[256]{0:T(256)S(1)}, f32[256]{0:T(256)}, u32[]{:S(2)}) copy-start(f32[256]{0:T(256)} %copy-done.151) | copy-start | bytes 3076
  666.6 137.3 %copy-start.158 = (f32[256]{0:T(256)S(1)}, f32[256]{0:T(256)}, u32[]{:S(2)}) copy-start(f32[256]{0:T(256)} %copy-done.157) | copy-start | bytes 3076
  666.7 137.4 %copy-start.160 = (f32[256]{0:T(256)S(1)}, f32[256]{0:T(256)}, u32[]{:S(2)}) copy-start(f32[256]{0:T(256)} %copy-done.159) | copy-start | bytes 3076
  807.7 65.8 %all-gather.27.cloned.1.call-start = ((), (), s32[]{:S(2)}) async-start(), calls=%async_computation.30 | async-start | bytes 1638400 | tf_op jit(solution)/shard_map/all_gather | solution.py:239
  821.6 188.0 %reduce-scatter.49.cloned.1.call-start = ((), (), s32[]{:S(2)}) async-start(), calls=%async_computation.43 | async-start | bytes 1474560
  972.6 70.6 %reduce-scatter.37.cloned.1.call-start = ((), (), s32[]{:S(2)}) async-start(), calls=%async_computation.35 | async-start | bytes 1638400 | tf_op jit(solution)/shard_map/reduce_scatter | solution.py:265
  976.1 99.3 %reduce-scatter.41.cloned.1.call-start = ((), (), s32[]{:S(2)}) async-start(), calls=%async_computation.39 | async-start | bytes 1638400 | tf_op jit(solution)/shard_map/reduce_scatter | solution.py:265
  978.4 129.3 %reduce-scatter.33.cloned.1.call-start = ((), (), s32[]{:S(2)}) async-start(), calls=%async_computation.31 | async-start | bytes 1638400 | tf_op jit(solution)/shard_map/reduce_scatter | solution.py:265
  980.7 174.2 %reduce-scatter.45.cloned.1.call-start = ((), (), s32[]{:S(2)}) async-start(), calls=%async_computation.41 | async-start | bytes 1843200 | tf_op jit(solution)/shard_map/reduce_scatter | solution.py:287
  988.3 203.8 %reduce-scatter.47.cloned.1.call-start = ((), (), s32[]{:S(2)}) async-start(), calls=%async_computation.42 | async-start | bytes 1843200 | tf_op jit(solution)/shard_map/reduce_scatter | solution.py:288
  995.4 235.0 %reduce-scatter.43.cloned.1.call-start = ((), (), s32[]{:S(2)}) async-start(), calls=%async_computation.40 | async-start | bytes 737280 | tf_op jit(solution)/shard_map/reduce_scatter | solution.py:286
  1001.3 106.4 %copy-start.130 = (f32[256]{0:T(256)S(1)}, f32[256]{0:T(256)}, u32[]{:S(2)}) copy-start(f32[256]{0:T(256)} %copy-done.129) | copy-start | bytes 3076
  1001.3 106.4 %copy-start.136 = (f32[256]{0:T(256)S(1)}, f32[256]{0:T(256)}, u32[]{:S(2)}) copy-start(f32[256]{0:T(256)} %copy-done.135) | copy-start | bytes 3076
  1002.7 147.9 %copy-start.31 = (f32[256,640]{1,0:T(8,128)S(1)}, f32[256,640]{1,0:T(8,128)}, u32[]{:S(2)}) copy-start(f32[256,640]{1,0:T(8,128)} %copy-done.30) | copy-start | bytes 1966084
  1002.8 149.2 %copy-start.27 = (f32[256,640]{1,0:T(8,128)S(1)}, f32[256,640]{1,0:T(8,128)}, u32[]{:S(2)}) copy-start(f32[256,640]{1,0:T(8,128)} %copy-done.26) | copy-start | bytes 1966084
  1002.8 149.2 %copy-start.29 = (f32[256,640]{1,0:T(8,128)S(1)}, f32[256,640]{1,0:T(8,128)}, u32[]{:S(2)}) copy-start(f32[256,640]{1,0:T(8,128)} %get-tuple-element.104) | copy-start | bytes 1966084
  1043.2 108.8 %copy-start.72 = (bf16[256,640]{1,0:T(8,128)(2,1)S(1)}, bf16[256,640]{1,0:T(8,128)(2,1)}, u32[]{:S(2)}) copy-start(bf16[256,640]{1,0:T(8,128)(2,1)} %reduce-scatter.37.cloned.1.call-done) | copy-start | bytes 983044
  (165 other events, 2102.3 us)
Sparse Core Ops, SparseCore 0:
  12.7 35.3 all-gather.20
  50.2 31.6 all-gather.16
  84.1 31.6 all-gather.12
  144.5 51.0 reduce-scatter.18
  197.8 51.7 reduce-scatter.22
  251.8 51.7 reduce-scatter.26
  307.8 32.3 all-gather.18
  341.8 31.6 all-gather.28
  375.1 31.6 all-gather.22
  408.8 31.6 all-gather.14
  442.9 51.0 reduce-scatter.34
  496.2 30.8 reduce-scatter.24
  530.6 31.4 all-gather.32
  563.5 31.6 all-gather.24
  596.7 31.6 all-gather.30
  630.6 30.1 reduce-scatter.20
  662.9 29.9 reduce-scatter.28
  695.2 50.8 reduce-scatter.38
  748.4 51.7 reduce-scatter.30
  807.8 32.3 all-gather.34
  842.4 31.0 all-gather.26
  972.7 36.8 reduce-scatter.48
  1011.9 31.2 reduce-scatter.36
  1045.3 29.9 reduce-scatter.40
  1077.7 29.9 reduce-scatter.32
  1111.5 37.9 reduce-scatter.44
  1153.2 38.8 reduce-scatter.46
  1195.8 34.5 reduce-scatter.42
where the time goes:
time: 1240 us
  waiting for transfers between devices  734 us (59%)
  matrix products  238 us (19%)
  other arithmetic  122 us (10%)
  blocking collectives  85.2 us (7%)
  local copies, waits for them, and re-layouts  33.4 us (3%)
  between operations  21.4 us (2%)
    reduce_scatter x3, waiting for transfers between devices, shards(): lax.psum_scatter(contract_last(grad_up_pre, up_full), 'tensor', scatter_d...  134 us
    reduce_scatter x3, waiting for transfers between devices, shards(): lax.psum_scatter(contract_last(attended_low, mix_full), 'tensor', scatter...  118 us
    reduce_scatter x3, waiting for transfers between devices, shards(): lax.psum_scatter(jnp.einsum('sgc,sdc->gd', grad_qkv, attn_full, preferred...  96.2 us
    all_gather x3, waiting for transfers between devices, shards(): lax.all_gather(grad_top.astype(jnp.bfloat16), 'tensor', axis=0, tiled=True)  77 us
    all_gather x3, waiting for transfers between devices, shards(): lax.all_gather(second_out.astype(jnp.bfloat16), 'tensor', axis=0, tiled=T...  59.9 us
    reduce_scatter x3, waiting for transfers between devices, shards(): lax.psum_scatter(contract_last(hidden, down_full).astype(jnp.bfloat16), '...  57.4 us
    all_gather x3, waiting for transfers between devices, shards(): lax.all_gather(first_out.astype(jnp.bfloat16), 'tensor', axis=0, tiled=True)  56.5 us
    convert_element_type x3, other arithmetic, attend_back(): grad_scores = grad_scores.astype(jnp.bfloat16)  51.9 us
  transfers between devices with their start and end apart: 28, of which 25 were waited for; matrix products, arithmetic and copies ran while one was open for 19% of the time, Pallas kernels for 0%

commit v1 on v0

v1 whole, which is shorter than its diff:
```python
import functools

import jax
import jax.numpy as jnp
import numpy as np
from jax import lax
from jax.experimental import pallas as pl
from jax.experimental.pallas import tpu as pltpu
from jax.sharding import PartitionSpec as P

HEAD_DIM = 32
LANES = 128
PACK = LANES // HEAD_DIM
BLOCK = 256
VMEM = 60 * 2**20
BF = jnp.bfloat16
F32 = jnp.float32
NN = (((1,), (0,)), ((), ()))
NT = (((1,), (1,)), ((), ()))
TN = (((0,), (0,)), ((), ()))


def dot(left, right, dims=NN):
    return lax.dot_general(left, right, dims, preferred_element_type=F32)


def params():
    return pltpu.CompilerParams(vmem_limit_bytes=VMEM)


def cost(flops, moved, transcendentals=0):
    return pl.CostEstimate(flops=flops, bytes_accessed=moved, transcendentals=transcendentals)


def whole(shape):
    return pl.BlockSpec(shape, lambda *_: (0,) * len(shape))


def norm(values):
    centred = values - jnp.mean(values, -1, keepdims=True)
    factor = lax.rsqrt(jnp.mean(centred * centred, -1, keepdims=True) + 1e-05)
    return centred * factor, factor


def norm_back(gradient, unit_rows, factor, gain_row):
    scaled = gradient * gain_row
    return factor * (
        scaled
        - jnp.mean(scaled, -1, keepdims=True)
        - unit_rows * jnp.mean(scaled * unit_rows, -1, keepdims=True)
    )


def rotary_tables(rows):
    halfway = HEAD_DIM // 2
    frequency = (1.0 / 10000.0 ** (np.arange(halfway, dtype=np.float32) * 2.0 / HEAD_DIM)).astype(np.float32)
    angles = np.arange(rows, dtype=np.float32)[:, None] * frequency[None, :]
    cosine = np.tile(np.cos(angles), (1, LANES // halfway)).astype(np.float32)
    sine = np.sin(angles)
    sine = np.tile(np.concatenate([-sine, sine], 1), (1, PACK)).astype(np.float32)
    return jnp.asarray(cosine), jnp.asarray(sine)


def swap_halves(values):
    halfway = HEAD_DIM // 2
    lane = lax.broadcasted_iota(jnp.int32, values.shape, 1)
    return jnp.where(
        lane % HEAD_DIM < halfway,
        pltpu.roll(values, LANES - halfway, 1),
        pltpu.roll(values, halfway, 1),
    )


def project_kernel(place_ref, *refs, parts, width):
    blocks = refs[:parts]
    gain_ref, shift_ref, weight_ref, bias_ref, cos_ref, sin_ref, x_ref, normed_ref, qkv_ref = refs[parts:]
    rows = blocks[0].shape[0]
    slot = lax.shift_right_logical(jnp.int32(rows * parts), place_ref[0])
    for part in range(parts):
        start = pl.multiple_of(place_ref[1 + part], rows)
        here = pl.ds(start, rows)
        x = blocks[part][...]
        x_ref[here, :] = x
        unit_rows, _ = norm(x.astype(F32))
        normed = (unit_rows * gain_ref[...] + shift_ref[...]).astype(BF)
        normed_ref[here, :] = normed
        at = pl.ds(pl.multiple_of(lax.rem(start, slot), rows), rows)
        cosine, sine = cos_ref[at, :], sin_ref[at, :]
        for s in range(3):
            rows_out = dot(normed, weight_ref[:, s * width : (s + 1) * width])
            rows_out = rows_out + bias_ref[:, s * width : (s + 1) * width]
            if s == 2:
                qkv_ref[here, s * width : (s + 1) * width] = rows_out.astype(BF)
                continue
            for tile in range(width // LANES):
                piece = rows_out[:, tile * LANES : (tile + 1) * LANES]
                piece = piece * cosine + swap_halves(piece) * sine
                if s == 0:
                    piece = piece * HEAD_DIM ** (-0.5)
                column = s * width + tile * LANES
                qkv_ref[here, column : column + LANES] = piece.astype(BF)


def project(place, blocks, gain, shift, weight, bias, cosine, sine):
    parts = len(blocks)
    rows, width = blocks[0].shape
    total = rows * parts
    return pl.pallas_call(
        functools.partial(project_kernel, parts=parts, width=width),
        in_specs=[pl.BlockSpec(memory_space=pltpu.SMEM)] + [pl.BlockSpec(memory_space=pltpu.VMEM)] * (parts + 6),
        out_specs=[pl.BlockSpec(memory_space=pltpu.VMEM)] * 3,
        out_shape=[
            jax.ShapeDtypeStruct((total, width), BF),
            jax.ShapeDtypeStruct((total, width), BF),
            jax.ShapeDtypeStruct((total, 3 * width), BF),
        ],
        compiler_params=params(),
        cost_estimate=cost(6 * total * width * width, 12 * total * width),
        name="project",
    )(place, *blocks, gain, shift, weight, bias, cosine, sine)


def by_bucket(bucket, total, lens_ref, body):
    for code in range(3):
        count = 1 << code
        width = total // count
        step = 4 // count

        @pl.when(bucket == code)
        def _(count=count, width=width, step=step):
            if count == 1:
                body(0, width, lens_ref[0])
            else:

                @pl.loop(0, count)
                def _(index):
                    body(pl.multiple_of(index * width, width), width, lens_ref[step * index])


def attend_kernel(place_ref, lens_ref, q_ref, k_ref, v_ref, out_ref, log_ref):
    total = q_ref.shape[0]
    lane = lax.broadcasted_iota(jnp.int32, (1, LANES), 1)
    area = lane // HEAD_DIM
    sub = lane % HEAD_DIM

    def sequence(first, width, length):
        keys, values = k_ref[pl.ds(first, width), :], v_ref[pl.ds(first, width), :]
        position = lax.broadcasted_iota(jnp.int32, (width, 1), 0)
        hidden = jnp.where(position < length, 0.0, -1e30).astype(BF)
        for start in range(0, width, BLOCK):
            here = pl.ds(first + start, BLOCK)
            queries = q_ref[here, :]
            total_rows, highs = None, []
            for head in range(PACK):
                own = area == head
                extra = (area == (head + 1) % PACK) & (sub == 0)
                q_one = jnp.where(own, queries, jnp.where(extra, BF(1), BF(0)))
                k_one = jnp.where(extra, jnp.broadcast_to(hidden, keys.shape), keys)
                scores = dot(q_one, k_one, NT)
                high = jnp.max(scores, 1, keepdims=True)
                weights = jnp.exp(scores - high).astype(BF)
                v_one = jnp.concatenate(
                    [
                        jnp.where(own, values, BF(0)),
                        jnp.broadcast_to(jnp.where(own, BF(1), BF(0)), values.shape),
                    ],
                    1,
                )
                term = dot(weights, v_one)
                total_rows = term if total_rows is None else total_rows + term
                highs.append(high)
            high = highs[PACK - 1]
            for head in range(PACK - 1):
                high = jnp.where(area == head, highs[head], high)
            summed = total_rows[:, LANES:]
            out_ref[here, :] = (total_rows[:, :LANES] / summed).astype(BF)
            log_ref[here, :] = high + jnp.log(summed)

    by_bucket(place_ref[0], total, lens_ref, sequence)


def attend(place, lens, qkv):
    total = qkv.shape[0]
    tiles = qkv.shape[1] // 3 // LANES
    scalar = pl.BlockSpec(memory_space=pltpu.SMEM)

    def tile(which):
        return pl.BlockSpec((total, LANES), lambda j: (0, which * tiles + j))

    return pl.pallas_call(
        attend_kernel,
        grid=(tiles,),
        in_specs=[scalar, scalar, tile(0), tile(1), tile(2)],
        out_specs=[tile(0), tile(0)],
        out_shape=[
            jax.ShapeDtypeStruct((total, tiles * LANES), BF),
            jax.ShapeDtypeStruct((total, tiles * LANES), F32),
        ],
        compiler_params=params(),
        cost_estimate=cost(
            12 * tiles * PACK * total * total * 256, 12 * total * tiles * LANES, tiles * PACK * total * total
        ),
        name="attend",
    )(place, lens, qkv, qkv, qkv)


def split3(values):
    first = values.astype(BF)
    rest = values - first.astype(F32)
    second = rest.astype(BF)
    return first, second, (rest - second.astype(F32)).astype(BF)


def attend_back_kernel(
    place_ref, lens_ref, q_ref, k_ref, v_ref, out_ref, grad_ref, log_ref, cos_ref, sin_ref,
    dq_ref, dk_ref, dv_ref, q_extra, g_extra, dq_total, dk_total,
):
    total = q_ref.shape[0]
    lane = lax.broadcasted_iota(jnp.int32, (1, LANES), 1)
    area = lane // HEAD_DIM
    sub = lane % HEAD_DIM
    first, second, third = split3(-pltpu.roll(log_ref[...], HEAD_DIM, 1))
    q_extra[...] = jnp.where(
        sub == 0, first, jnp.where(sub == 1, second, jnp.where(sub == 2, third, jnp.where(sub == 3, BF(1), BF(0))))
    )
    product = grad_ref[...].astype(F32) * out_ref[...].astype(F32)
    row_area = lax.broadcasted_iota(jnp.int32, (LANES, LANES), 0) // HEAD_DIM
    column_area = lax.broadcasted_iota(jnp.int32, (LANES, LANES), 1) // HEAD_DIM
    spread = jnp.where((row_area + 1) % PACK == column_area, 1.0, 0.0).astype(BF)
    delta = sum(dot(piece, spread) for piece in split3(product))
    first, second, third = split3(-delta)
    g_extra[...] = jnp.where(sub == 0, first, jnp.where(sub == 1, second, jnp.where(sub == 2, third, BF(0))))

    def sequence(begin, width, length):
        keys, values = k_ref[pl.ds(begin, width), :], v_ref[pl.ds(begin, width), :]
        position = lax.broadcasted_iota(jnp.int32, (width, 1), 0)
        hidden = jnp.where(position < length, 0.0, -1e30).astype(BF)
        k_extra = jnp.where(
            sub < 3, BF(1), jnp.where(sub == 3, jnp.broadcast_to(hidden, keys.shape), BF(0))
        )
        v_extra = jnp.broadcast_to(jnp.where(sub < 3, BF(1), BF(0)), values.shape)
        dv = jnp.zeros((width, LANES), F32)
        dk = jnp.zeros((width, LANES), F32)
        for start in range(0, width, BLOCK):
            here = pl.ds(begin + start, BLOCK)
            queries, grads = q_ref[here, :], grad_ref[here, :]
            q_more, g_more = q_extra[here, :], g_extra[here, :]
            dq = None
            for head in range(PACK):
                own, after = area == head, area == (head + 1) % PACK
                q_own, g_own = jnp.where(own, queries, BF(0)), jnp.where(own, grads, BF(0))
                k_one, v_one = jnp.where(own, keys, k_extra), jnp.where(own, values, v_extra)
                prob = jnp.exp(dot(k_one, jnp.where(after, q_more, q_own), NT))
                grad_prob = dot(v_one, jnp.where(after, g_more, g_own), NT)
                grad_scores = (prob * grad_prob).astype(BF)
                dv = dv + dot(prob.astype(BF), g_own)
                dk = dk + dot(grad_scores, q_own)
                term = dot(jnp.where(own, keys, BF(0)), grad_scores, TN)
                dq = term if dq is None else dq + term
            dq_total[here, :] = dq.T
        dv_ref[pl.ds(begin, width), :] = dv.astype(BF)
        dk_total[pl.ds(begin, width), :] = dk

    by_bucket(place_ref[0], total, lens_ref, sequence)
    slot = lax.shift_right_logical(jnp.int32(total), place_ref[0])
    for start in range(0, total, BLOCK):
        here = pl.ds(start, BLOCK)
        at = pl.ds(pl.multiple_of(lax.rem(jnp.int32(start), slot), BLOCK), BLOCK)
        cosine, sine = cos_ref[at, :], sin_ref[at, :]
        dq, dk = dq_total[here, :], dk_total[here, :]
        dq_ref[here, :] = ((dq * cosine - swap_halves(dq) * sine) * HEAD_DIM ** (-0.5)).astype(BF)
        dk_ref[here, :] = (dk * cosine - swap_halves(dk) * sine).astype(BF)


def attend_back(place, lens, qkv, attended, grad, log_total, cosine, sine):
    total = qkv.shape[0]
    tiles = qkv.shape[1] // 3 // LANES
    scalar = pl.BlockSpec(memory_space=pltpu.SMEM)

    def tile(which):
        return pl.BlockSpec((total, LANES), lambda j: (0, which * tiles + j))

    return pl.pallas_call(
        attend_back_kernel,
        grid=(tiles,),
        in_specs=[scalar, scalar, tile(0), tile(1), tile(2), tile(0), tile(0), tile(0)]
        + [whole((total, LANES))] * 2,
        out_specs=[tile(0)] * 3,
        out_shape=[jax.ShapeDtypeStruct((total, tiles * LANES), BF)] * 3,
        scratch_shapes=[pltpu.VMEM((total, LANES), BF)] * 2 + [pltpu.VMEM((total, LANES), F32)] * 2,
        compiler_params=params(),
        cost_estimate=cost(
            24 * tiles * PACK * total * total * 256, 20 * total * tiles * LANES, tiles * PACK * total * total
        ),
        name="attend_back",
    )(place, lens, qkv, qkv, qkv, attended, grad, log_total, cosine, sine)


def column_sums(values):
    return jnp.sum(values, 0, keepdims=True)


def feed_kernel(
    place_ref, x_ref, att_ref, grad_ref, weight_ref, gain_ref, shift_ref, out_bias_ref, up_bias_ref, down_bias_ref,
    up_ref, down_ref, mix_ref,
    layer_ref, residual_ref, grad_att_ref, sums_ref, grads_ref,
    normed, tops, mixes, atts, hidden, ups, *, row_steps, chunks,
):
    step = pl.program_id(0)
    rows, width = x_ref.shape

    @pl.when(step == 0)
    def _():
        sums_ref[...] = jnp.zeros_like(sums_ref)

    @pl.when(step < row_steps)
    def _():
        here = pl.ds(pl.multiple_of(step * rows, rows), rows)
        attended = att_ref[...]
        residual = x_ref[...].astype(F32) + dot(attended, mix_ref[...], NT) + out_bias_ref[...]
        unit_rows, factor = norm(residual)
        gain = gain_ref[...]
        second = (unit_rows * gain + shift_ref[...]).astype(BF)
        top = grad_ref[0].astype(F32) * weight_ref[...]
        top_low = top.astype(BF)
        normed[here, :] = second
        tops[here, :] = top_low
        atts[here, :] = attended
        below = jnp.zeros((rows, width), F32)
        grad_second = jnp.zeros((rows, width), F32)
        for chunk in range(chunks):
            columns = slice(chunk * width, (chunk + 1) * width)
            up_weight, down_weight = up_ref[:, columns], down_ref[:, columns]
            up = dot(second, up_weight) + up_bias_ref[:, columns]
            share = 0.5 * (1.0 + lax.erf(up * 0.7071067811865476))
            slope = share + up * jnp.exp(-0.5 * up * up) * 0.3989422804014327
            low = (up * share).astype(BF)
            hidden[here, columns] = low
            below = below + dot(low, down_weight, NT)
            grad_up = (dot(top_low, down_weight) * slope).astype(BF)
            ups[here, columns] = grad_up
            sums_ref[4 + chunk : 5 + chunk, :] += column_sums(grad_up.astype(F32))
            grad_second = grad_second + dot(grad_up, up_weight, NT)
        layer_ref[...] = (residual + below + down_bias_ref[...]).astype(BF)
        grad_residual = top + norm_back(grad_second, unit_rows, factor, gain)
        residual_ref[...] = grad_residual
        mixed = grad_residual.astype(BF)
        mixes[here, :] = mixed
        grad_att_ref[...] = dot(mixed, mix_ref[...]).astype(BF)
        sums_ref[0:1, :] += column_sums(grad_second * unit_rows)
        sums_ref[1:2, :] += column_sums(grad_second)
        sums_ref[2:3, :] += column_sums(grad_residual)
        sums_ref[3:4, :] += column_sums(top)

    for chunk in range(chunks):
        columns = slice(chunk * width, (chunk + 1) * width)

        @pl.when(step == row_steps + chunk)
        def _(columns=columns):
            grads_ref[...] = dot(normed[...], ups[:, columns], TN).astype(BF)

        @pl.when(step == row_steps + chunks + chunk)
        def _(columns=columns):
            grads_ref[...] = dot(tops[...], hidden[:, columns], TN).astype(BF)

    @pl.when(step == row_steps + 2 * chunks)
    def _():
        grads_ref[...] = dot(mixes[...], atts[...], TN).astype(BF)


def feed(place, x, attended, grad_blocks, row_weight, gain, shift, out_bias, up_bias, down_bias, weights):
    total, width = x.shape
    parts, rows = grad_blocks.shape[:2]
    hidden_width = up_bias.shape[1]
    chunks = hidden_width // width

    def last(i):
        return jnp.minimum(i, parts - 1)

    row = pl.BlockSpec((rows, width), lambda i, place: (last(i), 0))
    grid_spec = pltpu.PrefetchScalarGridSpec(
        num_scalar_prefetch=1,
        grid=(parts + 2 * chunks + 1,),
        in_specs=[
            row,
            row,
            pl.BlockSpec((1, rows, width), lambda i, place: (place[1 + last(i)] // rows, 0, 0)),
            pl.BlockSpec((rows, 1), lambda i, place: (last(i), 0)),
            whole((1, width)),
            whole((1, width)),
            whole((1, width)),
            whole((1, hidden_width)),
            whole((1, width)),
            pl.BlockSpec((width, hidden_width), lambda i, place: (0, 0), pipeline_mode=pl.Buffered(1)),
            pl.BlockSpec((width, hidden_width), lambda i, place: (0, 1), pipeline_mode=pl.Buffered(1)),
            pl.BlockSpec((width, width), lambda i, place: (0, 2 * chunks), pipeline_mode=pl.Buffered(1)),
        ],
        out_specs=[
            row,
            row,
            row,
            whole((16, width)),
            pl.BlockSpec((width, width), lambda i, place: (0, jnp.maximum(i - parts, 0))),
        ],
        scratch_shapes=[pltpu.VMEM((total, width), BF)] * 4 + [pltpu.VMEM((total, hidden_width), BF)] * 2,
    )
    return pl.pallas_call(
        functools.partial(feed_kernel, row_steps=parts, chunks=chunks),
        grid_spec=grid_spec,
        out_shape=[
            jax.ShapeDtypeStruct((total, width), BF),
            jax.ShapeDtypeStruct((total, width), F32),
            jax.ShapeDtypeStruct((total, width), BF),
            jax.ShapeDtypeStruct((16, width), F32),
            jax.ShapeDtypeStruct((width, (2 * chunks + 1) * width), BF),
        ],
        compiler_params=params(),
        cost_estimate=cost(6 * total * width * width * (2 * chunks + 1), 24 * width * hidden_width),
        name="feed",
    )(place, x, attended, grad_blocks, row_weight, gain, shift, out_bias, up_bias, down_bias, weights, weights, weights)


def project_grads_kernel(normed_ref, q_ref, k_ref, v_ref, out_ref, sums_ref):
    for s, ref in enumerate((q_ref, k_ref, v_ref)):

        @pl.when(pl.program_id(0) == s)
        def _(s=s, ref=ref):
            grads = ref[...]
            out_ref[...] = dot(normed_ref[...], grads, TN).astype(BF)
            sums_ref[s : s + 1, :] = column_sums(grads.astype(F32))


def project_grads(normed, grads):
    total, width = normed.shape
    return pl.pallas_call(
        project_grads_kernel,
        grid=(3,),
        in_specs=[whole((total, width))] * 4,
        out_specs=[pl.BlockSpec((width, width), lambda i: (0, i)), whole((8, width))],
        out_shape=[jax.ShapeDtypeStruct((width, 3 * width), BF), jax.ShapeDtypeStruct((8, width), F32)],
        compiler_params=params(),
        cost_estimate=cost(6 * total * width * width, 14 * total * width),
        name="project_grads",
    )(normed, *grads)


def project_back_kernel(q_ref, k_ref, v_ref, weight_ref, x_ref, residual_ref, gain_ref, out_ref, sums_ref):
    width = x_ref.shape[1]

    @pl.when(pl.program_id(0) == 0)
    def _():
        sums_ref[...] = jnp.zeros_like(sums_ref)

    grad_first = sum(
        dot(ref[...], weight_ref[:, s * width : (s + 1) * width], NT) for s, ref in enumerate((q_ref, k_ref, v_ref))
    )
    unit_rows, factor = norm(x_ref[...].astype(F32))
    out_ref[...] = (residual_ref[...] + norm_back(grad_first, unit_rows, factor, gain_ref[...])).astype(BF)
    sums_ref[0:1, :] += column_sums(grad_first * unit_rows)
    sums_ref[1:2, :] += column_sums(grad_first)


def project_back(grads, weight, x, grad_residual, gain):
    total, width = x.shape
    row = pl.BlockSpec((BLOCK, width), lambda i: (i, 0))
    return pl.pallas_call(
        project_back_kernel,
        grid=(total // BLOCK,),
        in_specs=[row, row, row, whole((width, 3 * width)), row, row, whole((1, width))],
        out_specs=[row, whole((8, width))],
        out_shape=[jax.ShapeDtypeStruct((total, width), BF), jax.ShapeDtypeStruct((8, width), F32)],
        compiler_params=params(),
        cost_estimate=cost(6 * total * width * width, 16 * total * width),
        name="project_back",
    )(*grads, weight, x, grad_residual, gain)


def shards(
    inputs,
    grad_out,
    masked,
    bucket,
    lengths,
    first_gain,
    first_shift,
    second_gain,
    second_shift,
    qkv_weight,
    qkv_bias,
    out_weight,
    out_bias,
    up_weight,
    up_bias,
    down_weight,
    down_bias,
):
    parts = lax.axis_size("tensor")
    dp_parts = lax.axis_size("dp")
    here = lax.axis_index("tensor")
    dp_here = lax.axis_index("dp")
    micro_total, rows, width = inputs.shape
    total = rows * parts
    assert micro_total <= parts
    spare = parts - micro_total
    first = (dp_here % 2) * spare
    micro = here - first
    working = (micro >= 0) & (micro < micro_total)
    micro_at = jnp.clip(micro, 0, micro_total - 1)

    def pairs(shift, towards):
        out = []
        for r in range(dp_parts):
            for t in range(parts):
                u = (t + shift) % parts
                owner = (u if towards else t) - (r % 2) * spare
                if 0 <= owner < micro_total:
                    out.append((r * parts + t, r * parts + u))
        return out

    def collect(array):
        blocks = [lax.dynamic_index_in_dim(array, micro_at, 0, False)]
        for shift in range(1, parts):
            target = lax.rem(here + shift, parts)
            sent = lax.dynamic_index_in_dim(array, jnp.clip(target - first, 0, micro_total - 1), 0, False)
            blocks.append(lax.ppermute(sent, ("dp", "tensor"), pairs(shift, True)))
        return blocks

    def give_back(array):
        split = array.reshape(parts, rows, width)
        blocks = [lax.dynamic_index_in_dim(split, here, 0, False)]
        for shift in range(1, parts):
            sent = lax.dynamic_index_in_dim(split, lax.rem(here + shift, parts), 0, False)
            blocks.append(lax.ppermute(sent, ("dp", "tensor"), pairs(shift, False)))
        blocks = jnp.stack(blocks)
        return jnp.stack(
            [
                lax.dynamic_index_in_dim(blocks, lax.rem(here - first - m + parts, parts), 0, False)
                for m in range(micro_total)
            ]
        )

    def sum_everywhere(values):
        for axis, size in (("dp", dp_parts), ("tensor", parts)):
            bit = 1
            while bit < size:
                values = values + lax.ppermute(values, axis, [(i, i ^ bit) for i in range(size)])
                bit *= 2
        return values

    rows_w = qkv_weight.shape[1]
    attn = lax.all_gather(qkv_weight, "tensor", axis=0)
    attn = attn.transpose(2, 1, 0, 3).reshape(rows_w, 3 * width)
    attn = lax.all_gather(attn, "dp", axis=0, tiled=True)
    rest = jnp.concatenate([up_weight, down_weight, out_weight], 1)
    cols_ffn, cols_attn = up_weight.shape[1], out_weight.shape[1]
    rest = lax.all_gather(rest, "tensor", axis=0)
    rest = jnp.concatenate(
        [
            rest[:, :, :cols_ffn].transpose(1, 0, 2).reshape(rows_w, -1),
            rest[:, :, cols_ffn : 2 * cols_ffn].transpose(1, 0, 2).reshape(rows_w, -1),
            rest[:, :, 2 * cols_ffn :].transpose(1, 0, 2).reshape(rows_w, -1),
        ],
        1,
    )
    rest = lax.all_gather(rest, "dp", axis=0, tiled=True)

    code = jnp.where(working, lax.dynamic_index_in_dim(bucket, micro_at, 0, False)[0], 2).astype(jnp.int32)
    lens = lax.dynamic_index_in_dim(lengths, micro_at, 0, False)
    chosen = lax.dynamic_index_in_dim(masked, micro_at, 0, False)
    sources = lax.rem(here - jnp.arange(parts, dtype=jnp.int32) + parts, parts)
    place = jnp.concatenate([code[None], sources * rows]).astype(jnp.int32)
    row_ids = jnp.arange(total, dtype=jnp.int32)
    position = row_ids % (jnp.int32(total) // jnp.left_shift(jnp.int32(1), code))
    slot = (row_ids - position) // (total // 4)
    length_row = jnp.sum(jnp.where(slot[:, None] == jnp.arange(4)[None, :], lens[None, :], 0), 1)
    counted = jnp.where((position < length_row) & working, chosen, 0).astype(F32)
    row_weight = counted * (3.0 * total / 8.0 / jnp.maximum(jnp.sum(counted), 1.0))

    cosine, sine = rotary_tables(total)
    blocks = collect(inputs)
    grad_blocks = collect(grad_out)
    x, first_normed, qkv = project(
        place, blocks, first_gain[None], first_shift[None], attn, qkv_bias.reshape(1, -1), cosine, sine
    )
    attended, log_total = attend(place, lens, qkv)
    layer, grad_residual, grad_attended, feed_sums, feed_grads = feed(
        place, x, attended, jnp.stack(grad_blocks), row_weight[:, None], second_gain[None], second_shift[None],
        out_bias[None], up_bias[None], down_bias[None], rest,
    )
    layer_out = give_back(layer)
    feed_grads = lax.psum_scatter(feed_grads, "dp", scatter_dimension=0, tiled=True)
    wide = 2 * cols_ffn * parts
    feed_grads = jnp.concatenate(
        [
            feed_grads[:, : wide // 2].reshape(rows_w, parts, cols_ffn),
            feed_grads[:, wide // 2 : wide].reshape(rows_w, parts, cols_ffn),
            feed_grads[:, wide:].reshape(rows_w, parts, cols_attn),
        ],
        2,
    ).transpose(1, 0, 2)
    feed_grads = lax.psum_scatter(feed_grads, "tensor", scatter_dimension=0, tiled=False).astype(F32)
    grads = attend_back(place, lens, qkv, attended, grad_attended, log_total, cosine, sine)
    attn_grads, bias_sums = project_grads(first_normed, grads)
    grad_in, first_sums = project_back(grads, attn, x, grad_residual, first_gain[None])
    grad_inputs = give_back(grad_in).astype(F32)
    attn_grads = lax.psum_scatter(attn_grads, "dp", scatter_dimension=0, tiled=True)
    attn_grads = attn_grads.reshape(rows_w, 3, parts, cols_attn).transpose(2, 1, 0, 3)
    attn_grads = lax.psum_scatter(attn_grads, "tensor", scatter_dimension=0, tiled=False).astype(F32)
    feed_sums = sum_everywhere(feed_sums)
    late_sums = sum_everywhere(jnp.concatenate([bias_sums[:3], first_sums[:2]]))
    return (
        layer_out,
        grad_inputs,
        attn_grads,
        feed_grads[:, 2 * cols_ffn :],
        feed_grads[:, :cols_ffn],
        feed_grads[:, cols_ffn : 2 * cols_ffn],
        late_sums[3],
        late_sums[4],
        feed_sums[0],
        feed_sums[1],
        late_sums[:3],
        feed_sums[2],
        feed_sums[4 : 4 + up_bias.shape[0] // width].reshape(-1),
        feed_sums[3],
    )


def solution(mesh):
    placed = (
        P(None, ("dp", "tensor"), None),
        P(None, ("dp", "tensor"), None),
        P(None, "dp"),
        P(None, "dp"),
        P(None, "dp"),
        P(),
        P(),
        P(),
        P(),
        P(None, "dp", "tensor"),
        P(),
        P("dp", "tensor"),
        P(),
        P("dp", "tensor"),
        P(),
        P("dp", "tensor"),
        P(),
    )
    return jax.shard_map(
        shards,
        mesh=mesh,
        in_specs=placed,
        out_specs=(
            P(None, ("dp", "tensor"), None),
            P(None, ("dp", "tensor"), None),
            P(None, "dp", "tensor"),
            P("dp", "tensor"),
            P("dp", "tensor"),
            P("dp", "tensor"),
            P(),
            P(),
            P(),
            P(),
            P(),
            P(),
            P(),
            P(),
        ),
        check_vma=False,
    )
```

time: 1240 us -> 478 us (0.39)
  waiting for transfers between devices: 734 us -> 177 us
  matrix products: 238 us -> 0 us
  Pallas kernels: 0 us -> 160 us
  other arithmetic: 122 us -> 18.6 us
  blocking collectives: 85.2 us -> 37.7 us
  starting transfers between devices: 2.83 us -> 37.9 us
    reduce_scatter x15 -> x4, waiting for transfers between devices: 482 us -> 113 us  [the longest x1 68.8 us: shards(): lax.psum_scatter(feed_grads, 'dp', scatter_dimension=0, tiled=True)]
    all_gather x12 -> x2, waiting for transfers between devices: 243 us -> 0.01 us  [the longest x1 0.01 us: shards(): attn = lax.all_gather(attn, 'dp', axis=0, tiled=True)]
    dot_general x51 -> x0, matrix products: 228 us -> none  [the longest x3 43.4 us: attend_back(): jnp.einsum('nqhe,nkhe->nhqk', grad_attended, values_low, preferred_elemen...]
    pallas_call x0 -> x6, Pallas kernels: none -> 160 us  [the longest x1 60.4 us: attend_back(): pl.pallas_call(attend_back_kernel, grid=(tiles,), in_specs=[scalar, scala...]
    ppermute x0 -> x22, waiting for transfers between devices: none -> 63.8 us  [the longest x10 35.2 us: sum_everywhere(): lax.ppermute(values, axis, [(i, i ^ bit) for i in range(size)])]
    convert_element_type x13 -> x3, other arithmetic: 62.5 us -> 4.01 us  [the longest x1 1.61 us: shards(): lax.psum_scatter(attn_grads, 'tensor', scatter_dimension=0, tiled=False)]
    psum x1 -> x0, blocking collectives: 40.6 us -> none  [shards(): lax.psum((gain_first, shift_first, gain_second, shift_second, qkv_bias_fu...]
    ppermute x0 -> x22, starting transfers between devices: none -> 37.7 us  [the longest x6 15.5 us: give_back(): blocks.append(lax.ppermute(sent, ('dp', 'tensor'), pairs(shift, False)))]
  transfers between devices with their start and end apart: 28 -> 28, of which waited for: 25 -> 10; matrix products, arithmetic and copies ran while one was open for 19% -> 8% of each run, Pallas kernels for 0% -> 10%
where the time goes in v1:
time: 478 us; the launch traced here: 470 us
  waiting for transfers between devices  177 us (37%)
  Pallas kernels  160 us (33%)
  starting transfers between devices  37.9 us (8%)
  blocking collectives  37.7 us (8%)
  local copies, waits for them, and re-layouts  22.2 us (5%)
  other arithmetic  18.6 us (4%)
  between operations  16.4 us (3%)
    reduce_scatter x1, waiting for transfers between devices, shards(): lax.psum_scatter(feed_grads, 'dp', scatter_dimension=0, tiled=True)  68.8 us
    pallas_call x1, Pallas kernels, attend_back(): pl.pallas_call(attend_back_kernel, grid=(tiles,), in_specs=[scalar, scala...  60.4 us
    pallas_call x1, Pallas kernels, feed(): pl.pallas_call(functools.partial(feed_kernel, row_steps=parts, chunks=chu...  45.3 us
    reduce_scatter x1, waiting for transfers between devices, shards(): lax.psum_scatter(attn_grads, 'dp', scatter_dimension=0, tiled=True)  44 us
    ppermute x10, waiting for transfers between devices, sum_everywhere(): lax.ppermute(values, axis, [(i, i ^ bit) for i in range(size)])  35.2 us
    pallas_call x1, Pallas kernels, attend(): pl.pallas_call(attend_kernel, grid=(tiles,), in_specs=[scalar, scalar, ti...  29.5 us
    all_gather x1, blocking collectives, shards(): rest = lax.all_gather(rest, 'tensor', axis=0)  20.4 us
    all_gather x1, blocking collectives, shards(): attn = lax.all_gather(qkv_weight, 'tensor', axis=0)  17.3 us
  transfers between devices with their start and end apart: 28, of which 10 were waited for; matrix products, arithmetic and copies ran while one was open for 8% of the time, Pallas kernels for 10%

profile of v1, /device:TPU:0, one launch (start us, length us, event | category | flops | bytes accessed | tf_op | source)
XLA Modules:
  0.0 470.2 jit_solution(15075343534703602270)
XLA Ops:
  7.3 17.3 %all-gather = bf16[12,80,160]{2,1,0:T(8,128)(2,1)S(1)} all-gather(bf16[3,80,160]{2,1,0:T(8,128)(2,1)} %param.28), channel_id=2, replica_groups=mesh['dp'=8,'tensor'=4] {'tensor'}, dimensions={0}, use_global_device_ids=true | all-gather | bytes 384000 | tf_op jit(solution)/shard_map/all_gather | solution.py:551
  24.9 1.1 reshape.140
  26.1 20.4 %all-gather.1 = bf16[320,1440]{1,0:T(8,128)(2,1)S(1)} all-gather(bf16[80,1440]{1,0:T(8,128)(2,1)S(1)} %pad_maximum_fusion.5), channel_id=3, replica_groups=mesh['dp'=8,'tensor'=4] {'tensor'}, dimensions={0}, use_global_device_ids=true | all-gather | bytes 1152000 | tf_op jit(solution)/shard_map/all_gather | solution.py:556
  47.3 1.0 pad_maximum_fusion.4
  49.6 2.0 collective-permute-start
  51.7 2.1 collective-permute-start.1
  54.6 2.5 collective-permute-start.3
  57.1 3.5 collective-permute-start.4
  60.6 1.3 collective-permute-start.5
  66.1 5.9 %convert_multiply_fusion.weight_ref = f32[1024,1]{1,0:T(8,128)} fusion(s32[1024,1]{1,0:T(8,128)S(1)} %copy.63, s32[1024,1]{1,0:T(8,128)S(1)} %copy.62, f32[]{:T(128)S(6)} %div.24, s32[]{:T(128)S(6)} %select_n.108, pred[]{:T(512)S(6)} %and.68, pred[]{:T(512)S(6)} %lt.88), kind=kLoop, calls=%fused_computation.9 | loop fusion | flops 12288 | bytes 12298 | tf_op jit(solution)/shard_map/mul | solution.py:577
  76.7 1.5 collective-permute-start.2
  78.8 6.3 %collective-permute-done.4 = bf16[256,640]{1,0:T(8,128)(2,1)} collective-permute-done((bf16[256,640]{1,0:T(8,128)(2,1)S(1)}, bf16[256,640]{1,0:T(8,128)(2,1)}, u32[]{:S(2)}, u32[]{:S(2)}) %collective-permute-start.4) | collective-permute-done | bytes 327712 | tf_op jit(solution)/shard_map/ppermute | solution.py:525
  85.1 2.4 pad_maximum_fusion.grad_ref
  87.4 7.0 %collective-permute-done.2.refs_3_ = bf16[256,640]{1,0:T(8,128)(2,1)S(1)} collective-permute-done((bf16[256,640]{1,0:T(8,128)(2,1)S(1)}, bf16[256,640]{1,0:T(8,128)(2,1)S(1)}, u32[]{:S(2)}, u32[]{:S(2)}) %collective-permute-start.2) | collective-permute-done | bytes 327712 | tf_op jit(solution)/shard_map/ppermute | solution.py:525
  95.2 8.9 %project.1 = (bf16[1024,640]{1,0:T(8,128)(2,1)}, bf16[1024,640]{1,0:T(8,128)(2,1)}, bf16[1024,1920]{1,0:T(8,128)(2,1)}) custom-call(s32[5]{0:T(128)} %pad_add_fusion.place_ref, bf16[256,640]{1,0:T(8,128)(2,1)} %get-tuple-element.76.refs_0_, bf16[256,640]{1,0:T(8,128)(2,1)} %collective-permute-done.refs_1_, bf16[256,640]{1,0:T(8,128)(2,1)} %collective-permute-done.1.refs_2_, ...), custom_call_target="tpu_custom_call" | custom-call | flops 2516582400 | bytes 7864320 | tf_op jit(solution)/shard_map/project/pallas_call | solution.py:108
  104.1 29.5 %attend.1 = (bf16[1024,640]{1,0:T(8,128)(2,1)}, f32[1024,640]{1,0:T(8,128)}) custom-call(s32[5]{0:T(128)} %pad_add_fusion.place_ref, s32[4]{0:T(128)} %copy-done.19, bf16[1024,1920]{1,0:T(8,128)(2,1)} %get-tuple-element.32.q_ref.k_ref.v_ref, bf16[1024,1920]{1,0:T(8,128)(2,1)} %get-tuple-element.32.q_ref.k_ref.v_ref, ...), custom_call_target="tpu_custom_call" | custom-call | flops 64424509440 | bytes 7864320 | tf_op jit(solution)/shard_map/attend/pallas_call | solution.py:190
  133.6 45.3 %feed.1 = (bf16[1024,640]{1,0:T(8,128)(2,1)}, f32[1024,640]{1,0:T(8,128)}, bf16[1024,640]{1,0:T(8,128)(2,1)}, f32[16,640]{1,0:T(8,128)}, bf16[640,5760]{1,0:T(8,128)(2,1)}) custom-call(s32[5]{0:T(128)} %pad_add_fusion.place_ref, bf16[1024,640]{1,0:T(8,128)(2,1)} %get-tuple-element.31.x_ref, bf16[1024,640]{1,0:T(8,128)(2,1)} %get-tuple-element.33.att_ref.out_ref, ...), custom_call_target="tpu_custom_call" | custom-call | flops 22649241600 | bytes 39321600 | tf_op jit(solution)/shard_map/feed/pallas_call | solution.py:407
  178.8 60.4 %attend_back.1 = (bf16[1024,640]{1,0:T(8,128)(2,1)}, bf16[1024,640]{1,0:T(8,128)(2,1)}, bf16[1024,640]{1,0:T(8,128)(2,1)}) custom-call(s32[5]{0:T(128)} %pad_add_fusion.place_ref, s32[4]{0:T(128)} %copy-done.19, bf16[1024,1920]{1,0:T(8,128)(2,1)} %get-tuple-element.32.q_ref.k_ref.v_ref, bf16[1024,1920]{1,0:T(8,128)(2,1)} %get-tuple-element.32.q_ref.k_ref.v_ref, ...), custom_call_target="tpu_custom_call" | custom-call | flops 128849018880 | bytes 13107200 | tf_op jit(solution)/shard_map/attend_back/pallas_call | solution.py:283
  239.2 7.3 %project_grads.1 = (bf16[640,1920]{1,0:T(8,128)(2,1)}, f32[8,640]{1,0:T(8,128)}) custom-call(bf16[1024,640]{1,0:T(8,128)(2,1)} %get-tuple-element.42.normed_ref, bf16[1024,640]{1,0:T(8,128)(2,1)} %get-tuple-element.37.q_ref, bf16[1024,640]{1,0:T(8,128)(2,1)} %get-tuple-element.38.k_ref, bf16[1024,640]{1,0:T(8,128)(2,1)} %get-tuple-element.39.v_ref), custom_call_target="tpu_custom_call" | custom-call | flops 2516582400 | bytes 9175040 | tf_op jit(solution)/shard_map/project_grads/pallas_call | solution.py:435
  247.3 44.0 %reduce-scatter.5.cloned.1.call-done = bf16[80,1920]{1,0:T(8,128)(2,1)} async-done(((bf16[640,1920]{1,0:T(8,128)(2,1)}), bf16[80,1920]{1,0:T(8,128)(2,1)}) %reduce-scatter.5.cloned.1.call-update) | async-done | bytes 307216 | tf_op jit(solution)/shard_map/reduce_scatter | solution.py:606
  291.3 1.4 reshape.147
  293.7 68.8 %reduce-scatter.9.cloned.1.call-done = bf16[80,5760]{1,0:T(8,128)(2,1)} async-done(((bf16[640,5760]{1,0:T(8,128)(2,1)}), bf16[80,5760]{1,0:T(8,128)(2,1)}) %reduce-scatter.9.cloned.1.call-update) | async-done | bytes 921616 | tf_op jit(solution)/shard_map/reduce_scatter | solution.py:591
  362.5 1.2 fusion.20
  364.0 1.1 maximum_bitcast_fusion
  365.1 9.0 %project_back.1 = (bf16[1024,640]{1,0:T(8,128)(2,1)}, f32[8,640]{1,0:T(8,128)}) custom-call(bf16[1024,640]{1,0:T(8,128)(2,1)} %get-tuple-element.37.q_ref, bf16[1024,640]{1,0:T(8,128)(2,1)} %get-tuple-element.38.k_ref, bf16[1024,640]{1,0:T(8,128)(2,1)} %get-tuple-element.39.v_ref, bf16[640,1920]{1,0:T(8,128)(2,1)} %all-gather.5.cloned.1.call-done.refs_6_.weight_ref, ...), custom_call_target="tpu_custom_call" | custom-call | flops 2516582400 | bytes 10485760 | tf_op jit(solution)/shard_map/project_back/pallas_call | solution.py:466
  374.8 1.5 collective-permute-start.18
  376.4 2.5 collective-permute-done.18
  378.9 1.4 collective-permute-start.19
  380.3 1.0 constant_dynamic-slice_fusion.7
  381.3 3.4 collective-permute-start.6
  384.7 1.5 collective-permute-start.20
  387.0 3.1 collective-permute-done.13
  390.8 3.1 collective-permute-done.14
  394.5 4.3 collective-permute-start.7
  398.8 1.9 collective-permute-start.8
  400.7 1.6 collective-permute-start.16
  402.4 1.4 collective-permute-start.21
  404.8 26.4 %collective-permute-done.16 = f32[5,640]{1,0:T(8,128)S(1)} collective-permute-done((f32[5,640]{1,0:T(8,128)S(1)}, f32[5,640]{1,0:T(8,128)S(1)}, u32[]{:S(2)}, u32[]{:S(2)}) %collective-permute-start.16) | collective-permute-done | bytes 12832 | tf_op jit(solution)/shard_map/ppermute | solution.py:546
  431.2 2.0 collective-permute-start.9
  433.8 1.9 collective-permute-start.10
  435.7 1.9 collective-permute-start.11
  439.7 10.8 %collective-permute-done.10 = bf16[256,640]{1,0:T(8,128)(2,1)} collective-permute-done((bf16[256,640]{1,0:T(8,128)(2,1)}, bf16[256,640]{1,0:T(8,128)(2,1)}, u32[]{:S(2)}, u32[]{:S(2)}) %collective-permute-start.10) | collective-permute-done | bytes 327712 | tf_op jit(solution)/shard_map/ppermute | solution.py:533
  450.5 4.5 collective-permute-done.11
  455.0 1.4 pad_maximum_fusion.2
  456.6 1.1 pad_maximum_fusion.3
  457.7 1.4 maximum_convert_fusion
  459.1 1.6 bitcast_convert_fusion.1
  460.7 1.0 bitcast_convert_fusion
  (139 shorter events, 22.1 us)
Async XLA Ops:
  7.2 57.2 %copy-start = (s32[3,1024]{1,0:T(4,128)S(1)}, s32[3,1024]{1,0:T(4,128)}, u32[]{:S(2)}) copy-start(s32[3,1024]{1,0:T(4,128)} %param.21) | copy-start | bytes 36868
  7.2 18.8 %copy-start.9 = (bf16[80,160]{1,0:T(8,128)(2,1)S(1)}, bf16[80,160]{1,0:T(8,128)(2,1)}, u32[]{:S(2)}) copy-start(bf16[80,160]{1,0:T(8,128)(2,1)} %param.30) | copy-start | bytes 76804
  7.2 18.8 %copy-start.7 = (bf16[80,640]{1,0:T(8,128)(2,1)S(1)}, bf16[80,640]{1,0:T(8,128)(2,1)}, u32[]{:S(2)}) copy-start(bf16[80,640]{1,0:T(8,128)(2,1)} %param.32) | copy-start | bytes 307204
  7.2 18.8 %copy-start.6 = (bf16[80,640]{1,0:T(8,128)(2,1)S(1)}, bf16[80,640]{1,0:T(8,128)(2,1)}, u32[]{:S(2)}) copy-start(bf16[80,640]{1,0:T(8,128)(2,1)} %param.34) | copy-start | bytes 307204
  7.2 87.2 %all-gather.5.cloned.1.call-start = ((), (), s32[]{:S(2)}) async-start(), calls=%async_computation.4 | async-start | bytes 2764800 | tf_op jit(solution)/shard_map/all_gather | solution.py:553
  25.9 107.6 %all-gather.7.cloned.1.call-start = ((), (), s32[]{:S(2)}) async-start(), calls=%async_computation.5 | async-start | bytes 8294400 | tf_op jit(solution)/shard_map/all_gather | solution.py:565
  47.2 1.5 copy-start.2
  48.3 243.1 %reduce-scatter.5.cloned.1.call-start = ((), (), s32[]{:S(2)}) async-start(), calls=%async_computation.6 | async-start | bytes 2764800 | tf_op jit(solution)/shard_map/reduce_scatter | solution.py:606
  48.8 5.0 %copy-start.3 = (bf16[3,256,640]{2,1,0:T(8,128)(2,1)S(1)}, bf16[3,256,640]{2,1,0:T(8,128)(2,1)}, u32[]{:S(2)}) copy-start(bf16[3,256,640]{2,1,0:T(8,128)(2,1)} %param.20) | copy-start | bytes 2949124
  49.6 37.8 %collective-permute-start = (bf16[256,640]{1,0:T(8,128)(2,1)S(1)}, bf16[256,640]{1,0:T(8,128)(2,1)}, u32[]{:S(2)}, u32[]{:S(2)}) collective-permute-start(bf16[256,640]{1,0:T(8,128)(2,1)S(1)} %get-tuple-element.75), channel_id=1, source_target_pairs={{0,1},{1,2},{3,0},{4,5},{5,6},{6,7},{8,9},{9,10},{11,8},{12,13},{1... | collective-permute-start | bytes 983048 | tf_op jit(solution)/shard_map/ppermute | solution.py:525
  51.7 10.2 %copy-start.21 = (s32[3,1]{0,1:T(1,128)S(1)}, s32[3,1]{0,1:T(1,128)}, u32[]{:S(2)}) copy-start(s32[3,1]{0,1:T(1,128)} %param.22) | copy-start | bytes 40
  51.7 35.8 %collective-permute-start.1 = (bf16[256,640]{1,0:T(8,128)(2,1)S(1)}, bf16[256,640]{1,0:T(8,128)(2,1)}, u32[]{:S(2)}, u32[]{:S(2)}) collective-permute-start(bf16[256,640]{1,0:T(8,128)(2,1)S(1)} %get-tuple-element.77), channel_id=1, source_target_pairs={{0,2},{2,0},{3,1},{4,6},{5,7},{7,5},{8,10},{10,8},{11,9},{12,14},{... | collective-permute-start | bytes 983048 | tf_op jit(solution)/shard_map/ppermute | solution.py:525
  54.6 22.1 %collective-permute-start.3 = (bf16[256,640]{1,0:T(8,128)(2,1)}, bf16[256,640]{1,0:T(8,128)(2,1)S(1)}, u32[]{:S(2)}, u32[]{:S(2)}) collective-permute-start(bf16[256,640]{1,0:T(8,128)(2,1)} %get-tuple-element.71), channel_id=1, source_target_pairs={{0,1},{1,2},{3,0},{4,5},{5,6},{6,7},{8,9},{9,10},{11,8},{12,13},{1... | collective-permute-start | bytes 983048 | tf_op jit(solution)/shard_map/ppermute | solution.py:525
  57.1 28.0 %collective-permute-start.4 = (bf16[256,640]{1,0:T(8,128)(2,1)S(1)}, bf16[256,640]{1,0:T(8,128)(2,1)}, u32[]{:S(2)}, u32[]{:S(2)}) collective-permute-start(bf16[256,640]{1,0:T(8,128)(2,1)S(1)} %get-tuple-element.73), channel_id=1, source_target_pairs={{0,2},{2,0},{3,1},{4,6},{5,7},{7,5},{8,10},{10,8},{11,9},{12,14},{... | collective-permute-start | bytes 983048 | tf_op jit(solution)/shard_map/ppermute | solution.py:525
  60.6 24.5 %collective-permute-start.5 = (bf16[256,640]{1,0:T(8,128)(2,1)S(1)}, bf16[256,640]{1,0:T(8,128)(2,1)}, u32[]{:S(2)}, u32[]{:S(2)}) collective-permute-start(bf16[256,640]{1,0:T(8,128)(2,1)S(1)} %get-tuple-element.72), channel_id=1, source_target_pairs={{1,0},{2,1},{3,2},{4,7},{6,5},{7,6},{9,8},{10,9},{11,10},{12,15},{... | collective-permute-start | bytes 983048 | tf_op jit(solution)/shard_map/ppermute | solution.py:525
  63.9 8.1 %copy-start.19 = (s32[4]{0:T(128)}, s32[4]{0:T(128)S(1)}, u32[]{:S(2)}) copy-start(s32[4]{0:T(128)S(1)} %fusion.17.lens_ref) | copy-start | bytes 52
  64.1 7.9 %copy-start.13 = (f32[640]{0:T(1024)S(1)}, f32[640]{0:T(1024)}, u32[]{:S(2)}) copy-start(f32[640]{0:T(1024)} %param.24) | copy-start | bytes 7684
  64.1 8.5 %copy-start.11 = (f32[3,640]{1,0:T(4,128)S(1)}, f32[3,640]{1,0:T(4,128)}, u32[]{:S(2)}) copy-start(f32[3,640]{1,0:T(4,128)} %param.29) | copy-start | bytes 23044
  64.1 9.1 %copy-start.14 = (f32[640]{0:T(1024)S(1)}, f32[640]{0:T(1024)}, u32[]{:S(2)}) copy-start(f32[640]{0:T(1024)} %param.25) | copy-start | bytes 7684
  64.1 9.6 %copy-start.10 = (f32[2560]{0:T(1024)S(1)}, f32[2560]{0:T(1024)}, u32[]{:S(2)}) copy-start(f32[2560]{0:T(1024)} %param.33) | copy-start | bytes 30724
  64.1 10.2 %copy-start.15 = (f32[640]{0:T(1024)S(1)}, f32[640]{0:T(1024)}, u32[]{:S(2)}) copy-start(f32[640]{0:T(1024)} %param.26) | copy-start | bytes 7684
  64.1 10.8 %copy-start.16 = (f32[640]{0:T(1024)S(1)}, f32[640]{0:T(1024)}, u32[]{:S(2)}) copy-start(f32[640]{0:T(1024)} %param.27) | copy-start | bytes 7684
  64.2 11.4 %copy-start.17 = (f32[640]{0:T(1024)S(1)}, f32[640]{0:T(1024)}, u32[]{:S(2)}) copy-start(f32[640]{0:T(1024)} %param.31) | copy-start | bytes 7684
  64.2 12.0 %copy-start.18 = (f32[640]{0:T(1024)S(1)}, f32[640]{0:T(1024)}, u32[]{:S(2)}) copy-start(f32[640]{0:T(1024)} %param.35) | copy-start | bytes 7684
  76.7 17.7 %collective-permute-start.2 = (bf16[256,640]{1,0:T(8,128)(2,1)S(1)}, bf16[256,640]{1,0:T(8,128)(2,1)S(1)}, u32[]{:S(2)}, u32[]{:S(2)}) collective-permute-start(bf16[256,640]{1,0:T(8,128)(2,1)S(1)} %get-tuple-element.74), channel_id=1, source_target_pairs={{1,0},{2,1},{3,2},{4,7},{6,5},{7,6},{9,8},{10,9},{11,10},{12,15},{... | collective-permute-start | bytes 983048 | tf_op jit(solution)/shard_map/ppermute | solution.py:525
  246.5 116.0 %reduce-scatter.9.cloned.1.call-start = ((), (), s32[]{:S(2)}) async-start(), calls=%async_computation.8 | async-start | bytes 8294400 | tf_op jit(solution)/shard_map/reduce_scatter | solution.py:591
  247.1 212.0 %reduce-scatter.7.cloned.1.call-start = ((), (), s32[]{:S(2)}) async-start(), calls=%async_computation.7 | async-start | bytes 614400 | tf_op jit(solution)/shard_map/reduce_scatter | solution.py:608
  247.3 127.5 %collective-permute-start.17 = (f32[16,640]{1,0:T(8,128)S(1)}, f32[16,640]{1,0:T(8,128)S(1)}, u32[]{:S(2)}, u32[]{:S(2)}) collective-permute-start(f32[16,640]{1,0:T(8,128)S(1)} %copy-done.8), channel_id=1, source_target_pairs={{0,4},{4,0},{8,12},{12,8},{16,20},{20,16},{24,28},{28,24},{1,5},{5... | collective-permute-start | bytes 122888 | tf_op jit(solution)/shard_map/ppermute | solution.py:546
  293.7 167.0 %reduce-scatter.11.cloned.1.call-start = ((), (), s32[]{:S(2)}) async-start(), calls=%async_computation.9 | async-start | bytes 1228800 | tf_op jit(solution)/shard_map/reduce_scatter | solution.py:601
  365.1 9.0 %copy-start.12 = (f32[8,640]{1,0:T(8,128)S(1)}, f32[8,640]{1,0:T(8,128)}, u32[]{:S(2)}) copy-start(f32[8,640]{1,0:T(8,128)} %get-tuple-element.45) | copy-start | bytes 61444
  365.1 15.2 %copy-start.5 = (bf16[1024,640]{1,0:T(8,128)(2,1)S(1)}, bf16[1024,640]{1,0:T(8,128)(2,1)}, u32[]{:S(2)}) copy-start(bf16[1024,640]{1,0:T(8,128)(2,1)} %get-tuple-element.34) | copy-start | bytes 3932164
  374.8 4.1 collective-permute-start.18
  376.3 10.0 %collective-permute-start.12 = (f32[5,640]{1,0:T(8,128)S(1)}, f32[5,640]{1,0:T(8,128)S(1)}, u32[]{:S(2)}, u32[]{:S(2)}) collective-permute-start(f32[5,640]{1,0:T(8,128)S(1)} %pad_maximum_fusion.6), channel_id=1, source_target_pairs={{0,4},{4,0},{8,12},{12,8},{16,20},{20,16},{24,28},{28,24},{1,5},{5... | collective-permute-start | bytes 38408 | tf_op jit(solution)/shard_map/ppermute | solution.py:546
  378.9 5.8 %collective-permute-start.19 = (f32[16,640]{1,0:T(8,128)S(1)}, f32[16,640]{1,0:T(8,128)S(1)}, u32[]{:S(2)}, u32[]{:S(2)}) collective-permute-start(f32[16,640]{1,0:T(8,128)S(1)} %add.172), channel_id=1, source_target_pairs={{0,16},{4,20},{8,24},{12,28},{16,0},{20,4},{24,8},{28,12},{1,17},{... | collective-permute-start | bytes 122888 | tf_op jit(solution)/shard_map/ppermute | solution.py:546
  380.3 23.5 %copy-start.4 = (bf16[1024,640]{1,0:T(8,128)(2,1)S(1)}, bf16[1024,640]{1,0:T(8,128)(2,1)}, u32[]{:S(2)}) copy-start(bf16[1024,640]{1,0:T(8,128)(2,1)} %get-tuple-element.41) | copy-start | bytes 3932164
  381.3 54.4 %collective-permute-start.6 = (bf16[256,640]{1,0:T(8,128)(2,1)}, bf16[256,640]{1,0:T(8,128)(2,1)S(1)}, u32[]{:S(2)}, u32[]{:S(2)}) collective-permute-start(bf16[256,640]{1,0:T(8,128)(2,1)} %get-tuple-element.67), channel_id=1, source_target_pairs={{0,1},{1,2},{2,3},{5,6},{6,7},{7,4},{8,9},{9,10},{10,11},{13,14},{... | collective-permute-start | bytes 983048 | tf_op jit(solution)/shard_map/ppermute | solution.py:533
  384.7 17.6 %collective-permute-start.20 = (f32[16,640]{1,0:T(8,128)S(1)}, f32[16,640]{1,0:T(8,128)S(1)}, u32[]{:S(2)}, u32[]{:S(2)}) collective-permute-start(f32[16,640]{1,0:T(8,128)S(1)} %add.173), channel_id=1, source_target_pairs={{0,1},{1,0},{2,3},{3,2},{4,5},{5,4},{6,7},{7,6},{8,9},{9,8},{10,11... | collective-permute-start | bytes 122888 | tf_op jit(solution)/shard_map/ppermute | solution.py:546
  386.3 3.8 collective-permute-start.13
  390.2 3.8 collective-permute-start.14
  393.9 6.8 %collective-permute-start.15 = (f32[5,640]{1,0:T(8,128)S(1)}, f32[5,640]{1,0:T(8,128)S(1)}, u32[]{:S(2)}, u32[]{:S(2)}) collective-permute-start(f32[5,640]{1,0:T(8,128)S(1)} %add.168), channel_id=1, source_target_pairs={{0,1},{1,0},{2,3},{3,2},{4,5},{5,4},{6,7},{7,6},{8,9},{9,8},{10,11... | collective-permute-start | bytes 38408 | tf_op jit(solution)/shard_map/ppermute | solution.py:546
  394.5 45.0 %collective-permute-start.7 = (bf16[256,640]{1,0:T(8,128)(2,1)}, bf16[256,640]{1,0:T(8,128)(2,1)S(1)}, u32[]{:S(2)}, u32[]{:S(2)}) collective-permute-start(bf16[256,640]{1,0:T(8,128)(2,1)} %get-tuple-element.66), channel_id=1, source_target_pairs={{0,2},{1,3},{2,0},{5,7},{6,4},{7,5},{8,10},{9,11},{10,8},{13,15},{... | collective-permute-start | bytes 983048 | tf_op jit(solution)/shard_map/ppermute | solution.py:533
  398.8 40.7 %collective-permute-start.8 = (bf16[256,640]{1,0:T(8,128)(2,1)S(1)}, bf16[256,640]{1,0:T(8,128)(2,1)S(1)}, u32[]{:S(2)}, u32[]{:S(2)}) collective-permute-start(bf16[256,640]{1,0:T(8,128)(2,1)S(1)} %get-tuple-element.65), channel_id=1, source_target_pairs={{0,3},{1,0},{2,1},{5,4},{6,5},{7,6},{8,11},{9,8},{10,9},{13,12},{1... | collective-permute-start | bytes 983048 | tf_op jit(solution)/shard_map/ppermute | solution.py:533
  400.7 30.4 %collective-permute-start.16 = (f32[5,640]{1,0:T(8,128)S(1)}, f32[5,640]{1,0:T(8,128)S(1)}, u32[]{:S(2)}, u32[]{:S(2)}) collective-permute-start(f32[5,640]{1,0:T(8,128)S(1)} %add.169), channel_id=1, source_target_pairs={{0,2},{1,3},{2,0},{3,1},{4,6},{5,7},{6,4},{7,5},{8,10},{9,11},{10,... | collective-permute-start | bytes 38408 | tf_op jit(solution)/shard_map/ppermute | solution.py:546
  402.4 31.4 %collective-permute-start.21 = (f32[16,640]{1,0:T(8,128)S(1)}, f32[16,640]{1,0:T(8,128)S(1)}, u32[]{:S(2)}, u32[]{:S(2)}) collective-permute-start(f32[16,640]{1,0:T(8,128)S(1)} %add.174), channel_id=1, source_target_pairs={{0,2},{1,3},{2,0},{3,1},{4,6},{5,7},{6,4},{7,5},{8,10},{9,11},{10,... | collective-permute-start | bytes 122888 | tf_op jit(solution)/shard_map/ppermute | solution.py:546
  431.2 8.6 %collective-permute-start.9 = (bf16[256,640]{1,0:T(8,128)(2,1)}, bf16[256,640]{1,0:T(8,128)(2,1)}, u32[]{:S(2)}, u32[]{:S(2)}) collective-permute-start(bf16[256,640]{1,0:T(8,128)(2,1)} %get-tuple-element.60), channel_id=1, source_target_pairs={{0,1},{1,2},{2,3},{5,6},{6,7},{7,4},{8,9},{9,10},{10,11},{13,14},{... | collective-permute-start | bytes 983048 | tf_op jit(solution)/shard_map/ppermute | solution.py:533
  433.8 16.7 %collective-permute-start.10 = (bf16[256,640]{1,0:T(8,128)(2,1)}, bf16[256,640]{1,0:T(8,128)(2,1)}, u32[]{:S(2)}, u32[]{:S(2)}) collective-permute-start(bf16[256,640]{1,0:T(8,128)(2,1)} %get-tuple-element.59), channel_id=1, source_target_pairs={{0,2},{1,3},{2,0},{5,7},{6,4},{7,5},{8,10},{9,11},{10,8},{13,15},{... | collective-permute-start | bytes 983048 | tf_op jit(solution)/shard_map/ppermute | solution.py:533
  435.7 19.3 %collective-permute-start.11 = (bf16[256,640]{1,0:T(8,128)(2,1)}, bf16[256,640]{1,0:T(8,128)(2,1)}, u32[]{:S(2)}, u32[]{:S(2)}) collective-permute-start(bf16[256,640]{1,0:T(8,128)(2,1)} %get-tuple-element.58), channel_id=1, source_target_pairs={{0,3},{1,0},{2,1},{5,4},{6,5},{7,6},{8,11},{9,8},{10,9},{13,12},{1... | collective-permute-start | bytes 983048 | tf_op jit(solution)/shard_map/ppermute | solution.py:533
  457.7 5.4 %copy-start.1 = (s32[3,1024]{1,0:T(4,128)S(1)}, s32[3,1024]{1,0:T(4,128)}, u32[]{:S(2)}) copy-start(s32[3,1024]{1,0:T(4,128)} %param.21) | copy-start | bytes 36868
  (3 other events, 2.7 us)
Sparse Core Ops, SparseCore 0:
  26.1 31.1 all-gather.4
  59.8 50.0 all-gather.6
  246.6 44.6 reduce-scatter.4
  294.7 67.7 reduce-scatter.8
  364.8 21.3 reduce-scatter.6
  388.3 36.4 reduce-scatter.10

commit v2 on v1

--- a/solution.py
+++ b/solution.py
@@ -71,56 +71,308 @@
     )
 
 
-def project_kernel(place_ref, *refs, parts, width):
-    blocks = refs[:parts]
-    gain_ref, shift_ref, weight_ref, bias_ref, cos_ref, sin_ref, x_ref, normed_ref, qkv_ref = refs[parts:]
+SCALARS = pl.BlockSpec(memory_space=pltpu.SMEM)
+LOCAL = pl.BlockSpec(memory_space=pltpu.VMEM)
+BESIDE = pl.BlockSpec(memory_space=pl.ANY)
+
+
+def shaped(shape, dtype=BF):
+    return jax.ShapeDtypeStruct(shape, dtype)
+
+
+def small_call(kernel, place, arrays, out_shape, name, after=()):
+    scalars = [] if place is None else [place]
+
+    def body(*refs):
+        place_ref, refs = (refs[0], refs[1:]) if scalars else (None, refs)
+        kernel(place_ref, refs[: len(arrays)], refs[len(arrays) + len(after) :])
+
+    return pl.pallas_call(
+        body,
+        in_specs=[SCALARS] * len(scalars) + [LOCAL] * len(arrays) + [BESIDE] * len(after),
+        out_specs=[LOCAL] * len(out_shape),
+        out_shape=out_shape,
+        compiler_params=params(),
+        cost_estimate=cost(0, 2 * sum(array.size * array.dtype.itemsize for array in arrays)),
+        name=name,
+    )(*scalars, *arrays, *after)
+
+
+def hold(arrays, after):
+    count = len(arrays)
+    return pl.pallas_call(
+        lambda *refs: None,
+        in_specs=[BESIDE] * (count + len(after)),
+        out_specs=[BESIDE] * count,
+        out_shape=[shaped(array.shape, array.dtype) for array in arrays],
+        input_output_aliases={index: index for index in range(count)},
+        name="hold",
+    )(*arrays, *after)
+
+
+def pick(place, array, parts, after=()):
+    micro_total, rows, width = array.shape
+
+    def kernel(place_ref, ins, outs):
+        for s in range(parts):
+            target = lax.rem(place_ref[1] + s, parts) - place_ref[4]
+            outs[s][...] = ins[0][jnp.clip(target, 0, micro_total - 1)]
+
+    return small_call(kernel, place, [array], [shaped((rows, width))] * parts, "pick", after)
+
+
+def put(place, blocks, micro_total, dtype):
+    parts = len(blocks)
+
+    def kernel(place_ref, ins, outs):
+        for m in range(micro_total):
+            shift = lax.rem(place_ref[1] - place_ref[4] - m + 2 * parts, parts)
+            for s in range(parts):
+
+                @pl.when(shift == s)
+                def _(m=m, s=s):
+                    outs[0][m] = ins[s][...].astype(dtype)
+
+    return small_call(kernel, place, blocks, [shaped((micro_total, *blocks[0].shape), dtype)], "put")[0]
+
+
+def join(arrays, after=()):
+    rows = arrays[0].shape[0]
+    columns = sum(array.shape[1] for array in arrays)
+
+    def kernel(place_ref, ins, outs):
+        column = 0
+        for ref in ins:
+            outs[0][:, column : column + ref.shape[1]] = ref[...]
+            column += ref.shape[1]
+
+    return small_call(kernel, None, arrays, [shaped((rows, columns))], "join", after)[0]
+
+
+def of_shift(values, shift):
+    found = values[0]
+    for s in range(1, len(values)):
+        found = jnp.where(shift == s, values[s], found)
+    return found
+
+
+def arrange(place, blocks, widths, after=()):
+    parts = len(blocks)
+    rows, columns = blocks[0].shape[-2], sum(widths)
+
+    def kernel(place_ref, ins, outs):
+        values = [ref[...] for ref in ins]
+        for owner in range(parts):
+            found = of_shift(values, lax.rem(place_ref[1] - owner + parts, parts))
+            column = at = 0
+            for index, width in enumerate(widths):
+                piece = found[index] if found.ndim == 3 else found[:, column : column + width]
+                outs[0][:, at + owner * width : at + (owner + 1) * width] = piece
+                column, at = column + width, at + parts * width
+
+    return small_call(kernel, place, blocks, [shaped((rows, parts * columns))], "arrange", after)[0]
+
+
+def split3(values):
+    first = values.astype(BF)
+    rest = values - first.astype(F32)
+    second = rest.astype(BF)
+    return first, second, (rest - second.astype(F32)).astype(BF)
+
+
+def write_split(ref, begin, values):
+    rows = values.shape[0]
+    for index, piece in enumerate(split3(values)):
+        ref[begin + index * rows : begin + (index + 1) * rows, : values.shape[1]] = piece
+
+
+def read_split(summed, begin, rows, columns):
+    return sum(summed[begin + index * rows : begin + (index + 1) * rows, :columns] for index in range(3))
+
+
+def sum_refs(refs):
+    summed = refs[0][...].astype(F32)
+    for ref in refs[1:]:
+        summed = summed + ref[...].astype(F32)
+    return summed
+
+
+def cut(summed, place_ref, outs, widths):
+    parts, rows = len(outs), summed.shape[0]
+    column = at = 0
+    for width in widths:
+        values = [summed[:, at + owner * width : at + (owner + 1) * width] for owner in range(parts)]
+        for s in range(parts):
+            outs[s][:rows, column : column + width] = of_shift(values, lax.rem(place_ref[1] + s, parts))
+        column, at = column + width, at + parts * width
+
+
+def deal(place, array, widths, parts):
+    rows = array.shape[0]
+
+    def kernel(place_ref, ins, outs):
+        cut(ins[0][...], place_ref, outs, widths)
+
+    return small_call(kernel, place, [array], [shaped((rows, sum(widths)))] * parts, "deal")
+
+
+def by_owner(place, array, widths, parts):
+    rows = array.shape[0]
+
+    def kernel(place_ref, ins, outs):
+        column = at = 0
+        for width in widths:
+            for owner in range(parts):
+                piece = ins[0][:, at + owner * width : at + (owner + 1) * width]
+                outs[0][owner, :, column : column + width] = piece
+            column, at = column + width, at + parts * width
+
+    return small_call(kernel, None, [array], [shaped((parts, rows, sum(widths)))], "by_owner")[0]
+
+
+def total_of(place, blocks, widths):
     rows = blocks[0].shape[0]
-    slot = lax.shift_right_logical(jnp.int32(rows * parts), place_ref[0])
-    for part in range(parts):
-        start = pl.multiple_of(place_ref[1 + part], rows)
-        here = pl.ds(start, rows)
-        x = blocks[part][...]
-        x_ref[here, :] = x
-        unit_rows, _ = norm(x.astype(F32))
-        normed = (unit_rows * gain_ref[...] + shift_ref[...]).astype(BF)
-        normed_ref[here, :] = normed
-        at = pl.ds(pl.multiple_of(lax.rem(start, slot), rows), rows)
-        cosine, sine = cos_ref[at, :], sin_ref[at, :]
-        for s in range(3):
-            rows_out = dot(normed, weight_ref[:, s * width : (s + 1) * width])
-            rows_out = rows_out + bias_ref[:, s * width : (s + 1) * width]
-            if s == 2:
-                qkv_ref[here, s * width : (s + 1) * width] = rows_out.astype(BF)
-                continue
-            for tile in range(width // LANES):
-                piece = rows_out[:, tile * LANES : (tile + 1) * LANES]
-                piece = piece * cosine + swap_halves(piece) * sine
-                if s == 0:
-                    piece = piece * HEAD_DIM ** (-0.5)
-                column = s * width + tile * LANES
-                qkv_ref[here, column : column + LANES] = piece.astype(BF)
-
-
-def project(place, blocks, gain, shift, weight, bias, cosine, sine):
+
+    def kernel(place_ref, ins, outs):
+        summed = sum_refs(ins)
+        column = 0
+        for out, width in zip(outs, widths):
+            out[...] = summed[:, column : column + width]
+            column += width
+
+    return small_call(kernel, place, blocks, [shaped((rows, width), F32) for width in widths], "total_of")
+
+
+def pair_sums(place, own, received, sums, sums_received):
+    count, rows, width = own.shape
+    extra = pl.cdiv(3 * sums.shape[0] * sums.shape[1] // width, 16) * 16
+    fold = width // sums.shape[1]
+
+    def kernel(place_ref, ins, outs):
+        shared = ins[2][...] + ins[3][...]
+        depth = shared.shape[0] // fold
+        shared = jnp.concatenate([shared[i * depth : (i + 1) * depth, :] for i in range(fold)], 1)
+        for index in range(count):
+            outs[index][:rows, :] = (ins[0][index].astype(F32) + ins[1][index].astype(F32)).astype(BF)
+            outs[index][rows:, :] = jnp.zeros((extra, width), BF)
+            write_split(outs[index], rows, shared)
+
+    return small_call(
+        kernel, place, [own, received, sums, sums_received], [shaped((rows + extra, width))] * count, "pair_sums"
+    )
+
+
+def plane_sums(place, blocks, widths, parts, rows, sums_shape):
+    width, depth = blocks[0].shape[1], sums_shape[0] * sums_shape[1] // blocks[0].shape[1]
+    columns = sum(widths)
+    fold = width // columns
+    extra = pl.cdiv(3 * depth * fold, 16) * 16
+
+    def kernel(place_ref, ins, outs):
+        summed = sum_refs(ins)
+        shared = read_split(summed, rows, depth, width)
+        shared = jnp.concatenate([shared[:, i * columns : (i + 1) * columns] for i in range(fold)], 0)
+        cut(summed[:rows, :].astype(BF), place_ref, outs, widths)
+        for out in outs:
+            out[rows:, :] = jnp.zeros((extra, columns), BF)
+            write_split(out, rows, shared)
+
+    return small_call(kernel, place, blocks, [shaped((rows + extra, columns))] * parts, "plane_sums")
+
+
+def last_sums(place, blocks, widths, rows, shared_rows):
+    columns = sum(widths)
+
+    def kernel(place_ref, ins, outs):
+        summed = sum_refs(ins)
+        column = 0
+        for index, width in enumerate(widths):
+            outs[0][index] = summed[:rows, column : column + width]
+            column += width
+        outs[1][...] = read_split(summed, rows, shared_rows, columns)
+
+    shapes = [shaped((len(widths), rows, widths[0]), F32), shaped((shared_rows, columns), F32)]
+    return small_call(kernel, place, blocks, shapes, "last_sums")
+
+
+def first_norm(place, blocks, gain, shift, near):
     parts = len(blocks)
     rows, width = blocks[0].shape
-    total = rows * parts
+
+    def kernel(place_ref, ins, outs):
+        gain_ref, shift_ref = ins[parts : parts + 2]
+        for index, ref in enumerate(ins[parts + 2 :]):
+            outs[2][index] = ref[...]
+        for s in range(parts):
+            here = pl.ds(pl.multiple_of(lax.rem(place_ref[1] - s + parts, parts) * rows, rows), rows)
+            x = ins[s][...]
+            outs[0][here, :] = x
+            unit_rows, _ = norm(x.astype(F32))
+            outs[1][here, :] = (unit_rows * gain_ref[...] + shift_ref[...]).astype(BF)
+
+    out_shape = [shaped((parts * rows, width))] * 2 + ([shaped((len(near), *near[0].shape))] if near else [])
+    return small_call(kernel, place, [*blocks, gain, shift, *near], out_shape, "first_norm")
+
+
+def project_kernel(place_ref, normed_ref, bias_ref, cos_ref, sin_ref, *refs, total, pieces):
+    weights, (qkv_ref, weight_ref) = refs[:pieces], refs[-2:]
+    rows, width = normed_ref.shape
+    step = pl.program_id(0)
+
+    @pl.when(step == 0)
+    def _():
+        if len(weights) == 1:
+            weight_ref[...] = weights[0][...]
+            return
+        half, depth, _ = weights[0].shape
+        for index in range(half):
+            for odd in range(2):
+                owner = jnp.bitwise_xor(place_ref[2], 2 * index + odd)
+                weight_ref[pl.ds(pl.multiple_of(owner * depth, depth), depth), :] = weights[odd][index]
+
+    slot = lax.shift_right_logical(jnp.int32(total), place_ref[0])
+    normed = normed_ref[...]
+    at = pl.ds(pl.multiple_of(lax.rem(step * rows, slot), rows), rows)
+    cosine, sine = cos_ref[at, :], sin_ref[at, :]
+    for s in range(3):
+        rows_out = dot(normed, weight_ref[:, s * width : (s + 1) * width])
+        rows_out = rows_out + bias_ref[:, s * width : (s + 1) * width]
+        if s == 2:
+            qkv_ref[:, s * width : (s + 1) * width] = rows_out.astype(BF)
+            continue
+        for tile in range(width // LANES):
+            piece = rows_out[:, tile * LANES : (tile + 1) * LANES]
+            piece = piece * cosine + swap_halves(piece) * sine
+            if s == 0:
+                piece = piece * HEAD_DIM ** (-0.5)
+            column = s * width + tile * LANES
+            qkv_ref[:, column : column + LANES] = piece.astype(BF)
+
+
+def project(place, normed, weights, bias, cosine, sine, after=()):
+    total, width = normed.shape
     return pl.pallas_call(
-        functools.partial(project_kernel, parts=parts, width=width),
-        in_specs=[pl.BlockSpec(memory_space=pltpu.SMEM)] + [pl.BlockSpec(memory_space=pltpu.VMEM)] * (parts + 6),
-        out_specs=[pl.BlockSpec(memory_space=pltpu.VMEM)] * 3,
-        out_shape=[
-            jax.ShapeDtypeStruct((total, width), BF),
-            jax.ShapeDtypeStruct((total, width), BF),
-            jax.ShapeDtypeStruct((total, 3 * width), BF),
-        ],
+        functools.partial(project_kernel, total=total, pieces=len(weights)),
+        grid=(total // BLOCK,),
+        in_specs=[
+            SCALARS,
+            pl.BlockSpec((BLOCK, width), lambda i: (i, 0)),
+            whole((1, 3 * width)),
+            whole((total, LANES)),
+            whole((total, LANES)),
+        ]
+        + [whole(weight.shape) for weight in weights]
+        + [BESIDE] * len(after),
+        out_specs=[pl.BlockSpec((BLOCK, 3 * width), lambda i: (i, 0)), whole((width, 3 * width))],
+        out_shape=[shaped((total, 3 * width)), shaped((width, 3 * width))],
         compiler_params=params(),
         cost_estimate=cost(6 * total * width * width, 12 * total * width),
         name="project",
-    )(place, *blocks, gain, shift, weight, bias, cosine, sine)
-
-
-def by_bucket(bucket, total, lens_ref, body):
+    )(place, normed, bias, cosine, sine, *weights, *after)
+
+
+def by_bucket(place_ref, total, lens_ref, body):
+    bucket, micro = place_ref[0], place_ref[3]
     for code in range(3):
         count = 1 << code
         width = total // count
@@ -129,12 +381,12 @@
         @pl.when(bucket == code)
         def _(count=count, width=width, step=step):
             if count == 1:
-                body(0, width, lens_ref[0])
+                body(0, width, lens_ref[micro, 0])
             else:
 
                 @pl.loop(0, count)
                 def _(index):
-                    body(pl.multiple_of(index * width, width), width, lens_ref[step * index])
+                    body(pl.multiple_of(index * width, width), width, lens_ref[micro, step * index])
 
 
 def attend_kernel(place_ref, lens_ref, q_ref, k_ref, v_ref, out_ref, log_ref):
@@ -176,7 +428,7 @@
             out_ref[here, :] = (total_rows[:, :LANES] / summed).astype(BF)
             log_ref[here, :] = high + jnp.log(summed)
 
-    by_bucket(place_ref[0], total, lens_ref, sequence)
+    by_bucket(place_ref, total, lens_ref, sequence)
 
 
 def attend(place, lens, qkv):
@@ -202,13 +454,6 @@
         ),
         name="attend",
     )(place, lens, qkv, qkv, qkv)
-
-
-def split3(values):
-    first = values.astype(BF)
-    rest = values - first.astype(F32)
-    second = rest.astype(BF)
-    return first, second, (rest - second.astype(F32)).astype(BF)
 
 
 def attend_back_kernel(
@@ -261,7 +506,7 @@
         dv_ref[pl.ds(begin, width), :] = dv.astype(BF)
         dk_total[pl.ds(begin, width), :] = dk
 
-    by_bucket(place_ref[0], total, lens_ref, sequence)
+    by_bucket(place_ref, total, lens_ref, sequence)
     slot = lax.shift_right_logical(jnp.int32(total), place_ref[0])
     for start in range(0, total, BLOCK):
         here = pl.ds(start, BLOCK)
@@ -300,18 +545,55 @@
     return jnp.sum(values, 0, keepdims=True)
 
 
+def row_weights(place_ref, lens_ref, masked_ref, total, groups_ratio=3.0 / 8.0):
+    micro = place_ref[3]
+    row = lax.broadcasted_iota(jnp.int32, (1, total), 1)
+    slot = lax.shift_right_logical(jnp.int32(total), place_ref[0])
+    position = jnp.bitwise_and(row, slot - 1)
+    begin = row - position
+    length = jnp.zeros((1, total), jnp.int32)
+    for index in range(4):
+        length = jnp.where(begin == index * (total // 4), lens_ref[micro, index], length)
+    chosen = masked_ref[pl.ds(micro, 1), :]
+    counted = jnp.where((position < length) & (place_ref[5] == 1), chosen, 0).astype(F32)
+    weights = counted * (groups_ratio * total / jnp.maximum(jnp.sum(counted), 1.0))
+    return jnp.broadcast_to(weights, (LANES, total)).T
+
+
 def feed_kernel(
-    place_ref, x_ref, att_ref, grad_ref, weight_ref, gain_ref, shift_ref, out_bias_ref, up_bias_ref, down_bias_ref,
-    up_ref, down_ref, mix_ref,
-    layer_ref, residual_ref, grad_att_ref, sums_ref, grads_ref,
-    normed, tops, mixes, atts, hidden, ups, *, row_steps, chunks,
+    place_ref, lens_ref, masked_ref, x_ref, att_ref, gain_ref, shift_ref, out_bias_ref, up_bias_ref, down_bias_ref,
+    *refs, row_steps, chunks, pieces,
 ):
+    pieces_refs, refs = refs[:pieces], refs[pieces:]
+    grad_refs, layer_refs = refs[:row_steps], refs[row_steps : 2 * row_steps]
+    residual_ref, grad_att_ref, sums_ref, grads_ref = refs[2 * row_steps : 2 * row_steps + 4]
+    normed, tops, mixes, atts, hidden, ups, weights, grad_rows, layer_rows, *held = refs[2 * row_steps + 4 :]
     step = pl.program_id(0)
     rows, width = x_ref.shape
+    table = held[0] if held else pieces_refs[0]
+    up_ref, down_ref = table.at[:, : chunks * width], table.at[:, chunks * width : 2 * chunks * width]
+    mix_ref = table.at[:, 2 * chunks * width :]
 
     @pl.when(step == 0)
     def _():
+        if held:
+            blocks, parts, depth, _ = pieces_refs[0].shape
+            share, mix_share = width * chunks // parts, width // parts
+            for block in range(blocks):
+                rows_at = slice(block * depth, (block + 1) * depth)
+                for part in range(parts):
+                    found = pieces_refs[0][block, part]
+                    up_ref[rows_at, part * share : (part + 1) * share] = found[:, :share]
+                    down_ref[rows_at, part * share : (part + 1) * share] = found[:, share : 2 * share]
+                    mix_ref[rows_at, part * mix_share : (part + 1) * mix_share] = found[:, 2 * share :]
         sums_ref[...] = jnp.zeros_like(sums_ref)
+        weights[...] = row_weights(place_ref, lens_ref, masked_ref, rows * row_steps)
+
+    for s in range(row_steps):
+
+        @pl.when((step < row_steps) & (lax.rem(place_ref[1] - step + 2 * row_steps, row_steps) == s))
+        def _(s=s):
+            grad_rows[...] = grad_refs[s][...]
 
     @pl.when(step < row_steps)
     def _():
@@ -321,7 +603,8 @@
         unit_rows, factor = norm(residual)
         gain = gain_ref[...]
         second = (unit_rows * gain + shift_ref[...]).astype(BF)
-        top = grad_ref[0].astype(F32) * weight_ref[...]
+        weight = weights[here, :]
+        top = grad_rows[...].astype(F32) * jnp.concatenate([weight] * (width // LANES), 1)
         top_low = top.astype(BF)
         normed[here, :] = second
         tops[here, :] = top_low
@@ -341,7 +624,7 @@
             ups[here, columns] = grad_up
             sums_ref[4 + chunk : 5 + chunk, :] += column_sums(grad_up.astype(F32))
             grad_second = grad_second + dot(grad_up, up_weight, NT)
-        layer_ref[...] = (residual + below + down_bias_ref[...]).astype(BF)
+        layer_rows[...] = (residual + below + down_bias_ref[...]).astype(BF)
         grad_residual = top + norm_back(grad_second, unit_rows, factor, gain)
         residual_ref[...] = grad_residual
         mixed = grad_residual.astype(BF)
@@ -352,6 +635,12 @@
         sums_ref[2:3, :] += column_sums(grad_residual)
         sums_ref[3:4, :] += column_sums(top)
 
+    for s in range(row_steps):
+
+        @pl.when((step < row_steps) & (lax.rem(step - place_ref[1] + row_steps, row_steps) == s))
+        def _(s=s):
+            layer_refs[s][...] = layer_rows[...]
+
     for chunk in range(chunks):
         columns = slice(chunk * width, (chunk + 1) * width)
 
@@ -368,86 +657,100 @@
         grads_ref[...] = dot(mixes[...], atts[...], TN).astype(BF)
 
 
-def feed(place, x, attended, grad_blocks, row_weight, gain, shift, out_bias, up_bias, down_bias, weights):
+def feed(place, lens, masked, x, attended, grad_blocks, gain, shift, out_bias, up_bias, down_bias, weights):
     total, width = x.shape
-    parts, rows = grad_blocks.shape[:2]
+    parts, rows = len(grad_blocks), grad_blocks[0].shape[0]
     hidden_width = up_bias.shape[1]
     chunks = hidden_width // width
-
-    def last(i):
-        return jnp.minimum(i, parts - 1)
-
-    row = pl.BlockSpec((rows, width), lambda i, place: (last(i), 0))
-    grid_spec = pltpu.PrefetchScalarGridSpec(
-        num_scalar_prefetch=1,
+    row = pl.BlockSpec((rows, width), lambda i: (jnp.minimum(i, parts - 1), 0))
+    once = pl.Buffered(1)
+    return pl.pallas_call(
+        functools.partial(feed_kernel, row_steps=parts, chunks=chunks, pieces=len(weights)),
         grid=(parts + 2 * chunks + 1,),
         in_specs=[
+            SCALARS,
+            SCALARS,
+            whole(masked.shape),
             row,
             row,
-            pl.BlockSpec((1, rows, width), lambda i, place: (place[1 + last(i)] // rows, 0, 0)),
-            pl.BlockSpec((rows, 1), lambda i, place: (last(i), 0)),
             whole((1, width)),
             whole((1, width)),
             whole((1, width)),
             whole((1, hidden_width)),
             whole((1, width)),
-            pl.BlockSpec((width, hidden_width), lambda i, place: (0, 0), pipeline_mode=pl.Buffered(1)),
-            pl.BlockSpec((width, hidden_width), lambda i, place: (0, 1), pipeline_mode=pl.Buffered(1)),
-            pl.BlockSpec((width, width), lambda i, place: (0, 2 * chunks), pipeline_mode=pl.Buffered(1)),
+        ]
+        + [pl.BlockSpec(weight.shape, lambda i, dims=weight.ndim: (0,) * dims, pipeline_mode=once) for weight in weights]
+        + [pl.BlockSpec((rows, width), lambda i: (0, 0), pipeline_mode=once)] * parts,
+        out_specs=[whole((rows, width))] * parts
+        + [row, row, whole((16, width)), pl.BlockSpec((width, width), lambda i: (0, jnp.maximum(i - parts, 0)))],
+        out_shape=[shaped((rows, width))] * parts
+        + [
+            shaped((total, width), F32),
+            shaped((total, width)),
+            shaped((16, width), F32),
+            shaped((width, (2 * chunks + 1) * width)),
         ],
-        out_specs=[
-            row,
-            row,
-            row,
-            whole((16, width)),
-            pl.BlockSpec((width, width), lambda i, place: (0, jnp.maximum(i - parts, 0))),
-        ],
-        scratch_shapes=[pltpu.VMEM((total, width), BF)] * 4 + [pltpu.VMEM((total, hidden_width), BF)] * 2,
-    )
-    return pl.pallas_call(
-        functools.partial(feed_kernel, row_steps=parts, chunks=chunks),
-        grid_spec=grid_spec,
-        out_shape=[
-            jax.ShapeDtypeStruct((total, width), BF),
-            jax.ShapeDtypeStruct((total, width), F32),
-            jax.ShapeDtypeStruct((total, width), BF),
-            jax.ShapeDtypeStruct((16, width), F32),
-            jax.ShapeDtypeStruct((width, (2 * chunks + 1) * width), BF),
-        ],
+        scratch_shapes=[pltpu.VMEM((total, width), BF)] * 4
+        + [pltpu.VMEM((total, hidden_width), BF)] * 2
+        + [pltpu.VMEM((total, LANES), F32)]
+        + [pltpu.VMEM((rows, width), BF)] * 2
+        + ([pltpu.VMEM((width, 2 * hidden_width + width), BF)] if weights[0].ndim == 4 else []),
         compiler_params=params(),
         cost_estimate=cost(6 * total * width * width * (2 * chunks + 1), 24 * width * hidden_width),
         name="feed",
-    )(place, x, attended, grad_blocks, row_weight, gain, shift, out_bias, up_bias, down_bias, weights, weights, weights)
-
-
-def project_grads_kernel(normed_ref, q_ref, k_ref, v_ref, out_ref, sums_ref):
+    )(place, lens, masked, x, attended, gain, shift, out_bias, up_bias, down_bias, *weights, *grad_blocks)
+
+
+def project_grads_kernel(place_ref, normed_ref, q_ref, k_ref, v_ref, *refs, pieces, skip):
+    outs, sums_ref = refs[skip:-1], refs[-1]
+    depth = normed_ref.shape[1] // pieces
     for s, ref in enumerate((q_ref, k_ref, v_ref)):
 
         @pl.when(pl.program_id(0) == s)
         def _(s=s, ref=ref):
             grads = ref[...]
-            out_ref[...] = dot(normed_ref[...], grads, TN).astype(BF)
+            found = dot(normed_ref[...], grads, TN).astype(BF)
             sums_ref[s : s + 1, :] = column_sums(grads.astype(F32))
-
-
-def project_grads(normed, grads):
+            if pieces == 1:
+                outs[0][...] = found
+                return
+            for piece in range(pieces):
+                block = found[piece * depth : (piece + 1) * depth, :]
+                offset = jnp.bitwise_xor(place_ref[2], piece)
+                for odd in range(2):
+
+                    @pl.when(lax.rem(offset, 2) == odd)
+                    def _(odd=odd, block=block, offset=offset):
+                        outs[odd][lax.shift_right_logical(offset, 1)] = block
+
+
+def project_grads(place, normed, grads, pieces, after):
     total, width = normed.shape
+    if pieces == 1:
+        outs = [pl.BlockSpec((width, width), lambda i: (0, i))]
+        shapes = [jax.ShapeDtypeStruct((width, 3 * width), BF)]
+    else:
+        half, depth = pieces // 2, width // pieces
+        outs = [pl.BlockSpec((half, depth, width), lambda i: (0, 0, i))] * 2
+        shapes = [jax.ShapeDtypeStruct((half, depth, 3 * width), BF)] * 2
     return pl.pallas_call(
-        project_grads_kernel,
+        functools.partial(project_grads_kernel, pieces=pieces, skip=len(after)),
         grid=(3,),
-        in_specs=[whole((total, width))] * 4,
-        out_specs=[pl.BlockSpec((width, width), lambda i: (0, i)), whole((8, width))],
-        out_shape=[jax.ShapeDtypeStruct((width, 3 * width), BF), jax.ShapeDtypeStruct((8, width), F32)],
+        in_specs=[SCALARS] + [whole((total, width))] * 4 + [BESIDE] * len(after),
+        out_specs=outs + [whole((8, width))],
+        out_shape=shapes + [jax.ShapeDtypeStruct((8, width), F32)],
         compiler_params=params(),
         cost_estimate=cost(6 * total * width * width, 14 * total * width),
         name="project_grads",
-    )(normed, *grads)
-
-
-def project_back_kernel(q_ref, k_ref, v_ref, weight_ref, x_ref, residual_ref, gain_ref, out_ref, sums_ref):
+    )(place, normed, *grads, *after)
+
+
+def project_back_kernel(place_ref, q_ref, k_ref, v_ref, weight_ref, x_ref, residual_ref, gain_ref, *refs, parts):
+    outs, sums_ref, found = refs[:parts], refs[parts], refs[parts + 1]
     width = x_ref.shape[1]
-
-    @pl.when(pl.program_id(0) == 0)
+    step = pl.program_id(0)
+
+    @pl.when(step == 0)
     def _():
         sums_ref[...] = jnp.zeros_like(sums_ref)
 
@@ -455,24 +758,31 @@
         dot(ref[...], weight_ref[:, s * width : (s + 1) * width], NT) for s, ref in enumerate((q_ref, k_ref, v_ref))
     )
     unit_rows, factor = norm(x_ref[...].astype(F32))
-    out_ref[...] = (residual_ref[...] + norm_back(grad_first, unit_rows, factor, gain_ref[...])).astype(BF)
+    found[...] = (residual_ref[...] + norm_back(grad_first, unit_rows, factor, gain_ref[...])).astype(BF)
     sums_ref[0:1, :] += column_sums(grad_first * unit_rows)
     sums_ref[1:2, :] += column_sums(grad_first)
-
-
-def project_back(grads, weight, x, grad_residual, gain):
+    for s in range(parts):
+
+        @pl.when(lax.rem(step - place_ref[1] + parts, parts) == s)
+        def _(s=s):
+            outs[s][...] = found[...]
+
+
+def project_back(place, grads, weight, x, grad_residual, gain, parts):
     total, width = x.shape
-    row = pl.BlockSpec((BLOCK, width), lambda i: (i, 0))
+    rows = total // parts
+    row = pl.BlockSpec((rows, width), lambda i: (i, 0))
     return pl.pallas_call(
-        project_back_kernel,
-        grid=(total // BLOCK,),
-        in_specs=[row, row, row, whole((width, 3 * width)), row, row, whole((1, width))],
-        out_specs=[row, whole((8, width))],
-        out_shape=[jax.ShapeDtypeStruct((total, width), BF), jax.ShapeDtypeStruct((8, width), F32)],
+        functools.partial(project_back_kernel, parts=parts),
+        grid=(parts,),
+        in_specs=[SCALARS, row, row, row, whole((width, 3 * width)), row, row, whole((1, width))],
+        out_specs=[whole((rows, width))] * parts + [whole((8, width))],
+        out_shape=[shaped((rows, width))] * parts + [shaped((8, width), F32)],
+        scratch_shapes=[pltpu.VMEM((rows, width), BF)],
         compiler_params=params(),
         cost_estimate=cost(6 * total * width * width, 16 * total * width),
         name="project_back",
-    )(*grads, weight, x, grad_residual, gain)
+    )(place, *grads, weight, x, grad_residual, gain)
 
 
 def shards(
@@ -517,111 +827,94 @@
                     out.append((r * parts + t, r * parts + u))
         return out
 
-    def collect(array):
-        blocks = [lax.dynamic_index_in_dim(array, micro_at, 0, False)]
-        for shift in range(1, parts):
-            target = lax.rem(here + shift, parts)
-            sent = lax.dynamic_index_in_dim(array, jnp.clip(target - first, 0, micro_total - 1), 0, False)
-            blocks.append(lax.ppermute(sent, ("dp", "tensor"), pairs(shift, True)))
-        return blocks
-
-    def give_back(array):
-        split = array.reshape(parts, rows, width)
-        blocks = [lax.dynamic_index_in_dim(split, here, 0, False)]
-        for shift in range(1, parts):
-            sent = lax.dynamic_index_in_dim(split, lax.rem(here + shift, parts), 0, False)
-            blocks.append(lax.ppermute(sent, ("dp", "tensor"), pairs(shift, False)))
-        blocks = jnp.stack(blocks)
-        return jnp.stack(
-            [
-                lax.dynamic_index_in_dim(blocks, lax.rem(here - first - m + parts, parts), 0, False)
-                for m in range(micro_total)
-            ]
-        )
-
-    def sum_everywhere(values):
-        for axis, size in (("dp", dp_parts), ("tensor", parts)):
-            bit = 1
-            while bit < size:
-                values = values + lax.ppermute(values, axis, [(i, i ^ bit) for i in range(size)])
-                bit *= 2
-        return values
-
-    rows_w = qkv_weight.shape[1]
-    attn = lax.all_gather(qkv_weight, "tensor", axis=0)
-    attn = attn.transpose(2, 1, 0, 3).reshape(rows_w, 3 * width)
-    attn = lax.all_gather(attn, "dp", axis=0, tiled=True)
-    rest = jnp.concatenate([up_weight, down_weight, out_weight], 1)
-    cols_ffn, cols_attn = up_weight.shape[1], out_weight.shape[1]
-    rest = lax.all_gather(rest, "tensor", axis=0)
-    rest = jnp.concatenate(
-        [
-            rest[:, :, :cols_ffn].transpose(1, 0, 2).reshape(rows_w, -1),
-            rest[:, :, cols_ffn : 2 * cols_ffn].transpose(1, 0, 2).reshape(rows_w, -1),
-            rest[:, :, 2 * cols_ffn :].transpose(1, 0, 2).reshape(rows_w, -1),
-        ],
-        1,
+    def to_owners(blocks):
+        return [blocks[0]] + [
+            lax.ppermute(blocks[shift], ("dp", "tensor"), pairs(shift, True)) for shift in range(1, parts)
+        ]
+
+    def from_owners(blocks):
+        return [blocks[0]] + [
+            lax.ppermute(blocks[shift], ("dp", "tensor"), pairs(shift, False)) for shift in range(1, parts)
+        ]
+
+    def shift_by(array, shift):
+        return lax.ppermute(array, "tensor", [(t, (t + shift) % parts) for t in range(parts)])
+
+    def swap_by(array, bits):
+        return lax.ppermute(array, "dp", [(r, r ^ bits) for r in range(dp_parts)])
+
+    rows_w, cols_ffn, cols_attn = qkv_weight.shape[1], up_weight.shape[1], out_weight.shape[1]
+    pieces = dp_parts if dp_parts == 8 else 1
+    code = jnp.where(working, lax.dynamic_index_in_dim(bucket, micro_at, 0, False)[0], 2)
+    place = jnp.stack([code, here, dp_here, micro_at, first, working]).astype(jnp.int32)
+
+    attn = [qkv_weight] + [shift_by(qkv_weight, shift) for shift in range(1, parts)]
+    blocks = to_owners(pick(place, inputs, parts, attn[1:2]))
+    attn = arrange(place, attn, (cols_attn,) * 3)
+    cosine, sine = rotary_tables(total)
+    rest = lax.all_gather(join([up_weight, down_weight, out_weight]), ("dp", "tensor"), axis=0)
+    rest = rest.reshape(dp_parts, parts, rows_w, -1)
+    if pieces == 1:
+        rest = rest.transpose(0, 2, 1, 3).reshape(width, parts, -1)
+        rest = jnp.split(rest, (cols_ffn, 2 * cols_ffn), 2)
+        rest = jnp.concatenate([piece.reshape(width, -1) for piece in rest], 1)
+        attn = [lax.all_gather(attn, "dp", axis=0, tiled=True)]
+        x, first_normed = first_norm(place, blocks, first_gain[None], first_shift[None], [])
+    else:
+        near = [attn] + [swap_by(attn, bits) for bits in range(2, pieces, 2)]
+        x, first_normed, near = first_norm(place, blocks, first_gain[None], first_shift[None], near)
+        attn = [near, swap_by(near, 1)]
+    qkv, attn = project(place, first_normed, attn, qkv_bias.reshape(1, -1), cosine, sine)
+    grad_blocks = to_owners(pick(place, grad_out, parts, (qkv,)))
+    attended, log_total = attend(place, lengths, qkv)
+    *layer, grad_residual, grad_attended, feed_sums, feed_grads = feed(
+        place, lengths, masked, x, attended, grad_blocks, second_gain[None], second_shift[None],
+        out_bias[None], up_bias[None], down_bias[None], [rest],
     )
-    rest = lax.all_gather(rest, "dp", axis=0, tiled=True)
-
-    code = jnp.where(working, lax.dynamic_index_in_dim(bucket, micro_at, 0, False)[0], 2).astype(jnp.int32)
-    lens = lax.dynamic_index_in_dim(lengths, micro_at, 0, False)
-    chosen = lax.dynamic_index_in_dim(masked, micro_at, 0, False)
-    sources = lax.rem(here - jnp.arange(parts, dtype=jnp.int32) + parts, parts)
-    place = jnp.concatenate([code[None], sources * rows]).astype(jnp.int32)
-    row_ids = jnp.arange(total, dtype=jnp.int32)
-    position = row_ids % (jnp.int32(total) // jnp.left_shift(jnp.int32(1), code))
-    slot = (row_ids - position) // (total // 4)
-    length_row = jnp.sum(jnp.where(slot[:, None] == jnp.arange(4)[None, :], lens[None, :], 0), 1)
-    counted = jnp.where((position < length_row) & working, chosen, 0).astype(F32)
-    row_weight = counted * (3.0 * total / 8.0 / jnp.maximum(jnp.sum(counted), 1.0))
-
-    cosine, sine = rotary_tables(total)
-    blocks = collect(inputs)
-    grad_blocks = collect(grad_out)
-    x, first_normed, qkv = project(
-        place, blocks, first_gain[None], first_shift[None], attn, qkv_bias.reshape(1, -1), cosine, sine
-    )
-    attended, log_total = attend(place, lens, qkv)
-    layer, grad_residual, grad_attended, feed_sums, feed_grads = feed(
-        place, x, attended, jnp.stack(grad_blocks), row_weight[:, None], second_gain[None], second_shift[None],
-        out_bias[None], up_bias[None], down_bias[None], rest,
-    )
-    layer_out = give_back(layer)
+    layer_out = put(place, from_owners(layer), micro_total, BF)
     feed_grads = lax.psum_scatter(feed_grads, "dp", scatter_dimension=0, tiled=True)
-    wide = 2 * cols_ffn * parts
-    feed_grads = jnp.concatenate(
-        [
-            feed_grads[:, : wide // 2].reshape(rows_w, parts, cols_ffn),
-            feed_grads[:, wide // 2 : wide].reshape(rows_w, parts, cols_ffn),
-            feed_grads[:, wide:].reshape(rows_w, parts, cols_attn),
-        ],
-        2,
-    ).transpose(1, 0, 2)
-    feed_grads = lax.psum_scatter(feed_grads, "tensor", scatter_dimension=0, tiled=False).astype(F32)
-    grads = attend_back(place, lens, qkv, attended, grad_attended, log_total, cosine, sine)
-    attn_grads, bias_sums = project_grads(first_normed, grads)
-    grad_in, first_sums = project_back(grads, attn, x, grad_residual, first_gain[None])
-    grad_inputs = give_back(grad_in).astype(F32)
-    attn_grads = lax.psum_scatter(attn_grads, "dp", scatter_dimension=0, tiled=True)
-    attn_grads = attn_grads.reshape(rows_w, 3, parts, cols_attn).transpose(2, 1, 0, 3)
-    attn_grads = lax.psum_scatter(attn_grads, "tensor", scatter_dimension=0, tiled=False).astype(F32)
-    feed_sums = sum_everywhere(feed_sums)
-    late_sums = sum_everywhere(jnp.concatenate([bias_sums[:3], first_sums[:2]]))
+    feed_grads = by_owner(place, feed_grads, (cols_ffn, cols_ffn, cols_attn), parts)
+    feed_grads = lax.psum_scatter(feed_grads, "tensor", scatter_dimension=0, tiled=False)
+    grad_up, grad_down, grad_mix = total_of(place, [feed_grads], (cols_ffn, cols_ffn, cols_attn))
+    grads = attend_back(place, lengths, qkv, attended, grad_attended, log_total, cosine, sine)
+    *attn_grads, bias_sums = project_grads(place, first_normed, grads, pieces, (layer_out,))
+    *grad_in, first_sums = project_back(place, grads, attn, x, grad_residual, first_gain[None], parts)
+    grad_inputs = put(place, from_owners(grad_in), micro_total, F32)
+    chunks = up_bias.shape[0] // width
+    sums = jnp.concatenate([feed_sums[: 4 + chunks], bias_sums[:3], first_sums[:2]])
+    sums = jnp.pad(sums, ((0, -sums.shape[0] % 3), (0, 0)))
+    if pieces == 1:
+        attn_grads = lax.psum_scatter(attn_grads[0], "dp", scatter_dimension=0, tiled=True)
+        attn_grads = deal(place, attn_grads, (cols_attn,) * 3, parts)
+        attn_grads = [attn_grads[0]] + [shift_by(attn_grads[shift], shift) for shift in range(1, parts)]
+        attn_grads = jnp.stack(total_of(place, attn_grads, (cols_attn,) * 3))
+        sums = jnp.sum(lax.all_gather(sums, ("dp", "tensor"), axis=0), 0)
+    else:
+        even, odd = attn_grads
+        both = pair_sums(place, even, swap_by(odd, 1), sums, swap_by(sums, 1))
+        both = [both[0]] + [swap_by(both[index], 2 * index) for index in range(1, pieces // 2)]
+        dealt = plane_sums(place, both, (cols_attn,) * 3, parts, rows_w, sums.shape)
+        dealt = [dealt[0]] + [shift_by(dealt[shift], shift) for shift in range(1, parts)]
+        shared_rows = sums.size // (3 * cols_attn)
+        attn_grads, shared = last_sums(place, dealt, (cols_attn,) * 3, rows_w, shared_rows)
+        fold = 3 * width // (3 * cols_attn)
+        shared = jnp.concatenate(jnp.split(shared, fold, 0), 1)
+        sums = jnp.concatenate(jnp.split(shared, 3, 1), 0)
+    feed_sums, late_sums = sums[: 4 + chunks], sums[4 + chunks :]
     return (
         layer_out,
         grad_inputs,
         attn_grads,
-        feed_grads[:, 2 * cols_ffn :],
-        feed_grads[:, :cols_ffn],
-        feed_grads[:, cols_ffn : 2 * cols_ffn],
+        grad_mix,
+        grad_up,
+        grad_down,
         late_sums[3],
         late_sums[4],
         feed_sums[0],
         feed_sums[1],
         late_sums[:3],
         feed_sums[2],
-        feed_sums[4 : 4 + up_bias.shape[0] // width].reshape(-1),
+        feed_sums[4:].reshape(-1),
         feed_sums[3],
     )
 

time: 478 us -> 335 us (0.70)
  waiting for transfers between devices: 177 us -> 76.1 us
  blocking collectives: 37.7 us -> 0 us
  starting transfers between devices: 37.9 us -> 69.9 us
  other arithmetic: 18.6 us -> 1.47 us
  Pallas kernels: 160 us -> 150 us
  local copies, waits for them, and re-layouts: 22.2 us -> 16.7 us
    reduce_scatter x2 -> x0, waiting for transfers between devices: 44 us -> none  [the longest x1 44 us: shards(): lax.psum_scatter(attn_grads, 'dp', scatter_dimension=0, tiled=True)]
    reduce_scatter x1, waiting for transfers between devices: 68.8 us -> 25.4 us  [shards(): lax.psum_scatter(feed_grads, 'dp', scatter_dimension=0, tiled=True)]
    all_gather x2 -> x0, blocking collectives: 37.7 us -> none  [the longest x1 20.4 us: shards(): rest = lax.all_gather(rest, 'tensor', axis=0)]
    ppermute x22 -> x27, starting transfers between devices: 37.7 us -> 69.7 us  [the longest x9 21.3 us: swap_by(): return lax.ppermute(array, 'dp', [(r, r ^ bits) for r in range(dp_parts)])]
    pallas_call x3 -> x15, Pallas kernels: 25.1 us -> 55.8 us  [the longest x12 30 us: small_call(): pl.pallas_call(body, in_specs=[SCALARS] * len(scalars) + [LOCAL] * len(ar...]
    pallas_call x1, Pallas kernels: 60.4 us -> 29.9 us  [attend_back(): pl.pallas_call(attend_back_kernel, grid=(tiles,), in_specs=[scalar, scala...]
    ppermute x22 -> x27, waiting for transfers between devices: 63.8 us -> 50.6 us  [the longest x9 23.8 us: swap_by(): return lax.ppermute(array, 'dp', [(r, r ^ bits) for r in range(dp_parts)])]
    pallas_call x1, Pallas kernels: 29.5 us -> 16.7 us  [attend(): pl.pallas_call(attend_kernel, grid=(tiles,), in_specs=[scalar, scalar, ti...]
  transfers between devices with their start and end apart: 28 -> 30, of which waited for: 10 -> 12; matrix products, arithmetic and copies ran while one was open for 8% -> 3% of each run, Pallas kernels for 10% -> 30%
where the time goes in v2:
time: 335 us; the launch traced here: 329 us
  Pallas kernels  150 us (45%)
  waiting for transfers between devices  76.1 us (23%)
  starting transfers between devices  69.9 us (21%)
  local copies, waits for them, and re-layouts  16.7 us (5%)
  between operations  15.1 us (5%)
    pallas_call x1, Pallas kernels, feed(): pl.pallas_call(functools.partial(feed_kernel, row_steps=parts, chunks=chu...  47.9 us
    pallas_call x12, Pallas kernels, small_call(): pl.pallas_call(body, in_specs=[SCALARS] * len(scalars) + [LOCAL] * len(ar...  30 us
    pallas_call x1, Pallas kernels, attend_back(): pl.pallas_call(attend_back_kernel, grid=(tiles,), in_specs=[scalar, scala...  29.9 us
    reduce_scatter x1, waiting for transfers between devices, shards(): lax.psum_scatter(feed_grads, 'dp', scatter_dimension=0, tiled=True)  25.4 us
    ppermute x9, waiting for transfers between devices, swap_by(): return lax.ppermute(array, 'dp', [(r, r ^ bits) for r in range(dp_parts)])  23.8 us
    ppermute x9, starting transfers between devices, swap_by(): return lax.ppermute(array, 'dp', [(r, r ^ bits) for r in range(dp_parts)])  21.3 us
    ppermute x6, starting transfers between devices, to_owners(): lax.ppermute(blocks[shift], ('dp', 'tensor'), pairs(shift, True))  19.7 us
    ppermute x6, starting transfers between devices, from_owners(): lax.ppermute(blocks[shift], ('dp', 'tensor'), pairs(shift, False))  16.8 us
  transfers between devices with their start and end apart: 30, of which 12 were waited for; matrix products, arithmetic and copies ran while one was open for 3% of the time, Pallas kernels for 30%

profile of v2, /device:TPU:0, one launch (start us, length us, event | category | flops | bytes accessed | tf_op | source)
XLA Modules:
  0.0 329.4 jit_solution(8574084619473874742)
XLA Ops:
  7.3 1.7 join.1
  9.0 4.1 %collective-permute-start.4 = (bf16[3,80,160]{2,1,0:T(8,128)(2,1)}, bf16[3,80,160]{2,1,0:T(8,128)(2,1)S(1)}, u32[]{:S(2)}, u32[]{:S(2)}) collective-permute-start(bf16[3,80,160]{2,1,0:T(8,128)(2,1)} %refs_1_.5), channel_id=1, source_target_pairs={{0,2},{1,3},{2,0},{3,1},{4,6},{5,7},{6,4},{7,5},{8,10},{9,11},{10,... | collective-permute-start | bytes 230408 | tf_op jit(solution)/shard_map/ppermute | solution.py:841
  13.1 1.6 collective-permute-start
  14.7 2.2 collective-permute-start.5
  18.8 3.9 %collective-permute-done.4.refs_3_ = bf16[3,80,160]{2,1,0:T(8,128)(2,1)S(1)} collective-permute-done((bf16[3,80,160]{2,1,0:T(8,128)(2,1)}, bf16[3,80,160]{2,1,0:T(8,128)(2,1)S(1)}, u32[]{:S(2)}, u32[]{:S(2)}) %collective-permute-start.4) | collective-permute-done | bytes 76832 | tf_op jit(solution)/shard_map/ppermute | solution.py:841
  24.1 2.0 arrange.1.refs_7_
  26.1 2.8 collective-permute-start.8
  28.9 2.4 pick.2
  31.3 4.3 %collective-permute-start.1 = (bf16[256,640]{1,0:T(8,128)(2,1)}, bf16[256,640]{1,0:T(8,128)(2,1)S(1)}, u32[]{:S(2)}, u32[]{:S(2)}) collective-permute-start(bf16[256,640]{1,0:T(8,128)(2,1)} %get-tuple-element.62), channel_id=1, source_target_pairs={{0,1},{1,2},{3,0},{4,5},{5,6},{6,7},{8,9},{9,10},{11,8},{12,13},{1... | collective-permute-start | bytes 983048 | tf_op jit(solution)/shard_map/ppermute | solution.py:832
  35.6 3.8 %collective-permute-start.2 = (bf16[256,640]{1,0:T(8,128)(2,1)}, bf16[256,640]{1,0:T(8,128)(2,1)S(1)}, u32[]{:S(2)}, u32[]{:S(2)}) collective-permute-start(bf16[256,640]{1,0:T(8,128)(2,1)} %get-tuple-element.63), channel_id=1, source_target_pairs={{0,2},{2,0},{3,1},{4,6},{5,7},{7,5},{8,10},{10,8},{11,9},{12,14},{... | collective-permute-start | bytes 983048 | tf_op jit(solution)/shard_map/ppermute | solution.py:832
  39.4 1.3 collective-permute-start.3
  41.0 1.1 collective-permute-start.6
  43.3 8.9 %collective-permute-done.7.refs_9_ = bf16[80,1920]{1,0:T(8,128)(2,1)S(1)} collective-permute-done((bf16[80,1920]{1,0:T(8,128)(2,1)}, bf16[80,1920]{1,0:T(8,128)(2,1)S(1)}, u32[]{:S(2)}, u32[]{:S(2)}) %collective-permute-start.7) | collective-permute-done | bytes 307232 | tf_op jit(solution)/shard_map/ppermute | solution.py:844
  52.1 3.6 %collective-permute-done.6.refs_8_ = bf16[80,1920]{1,0:T(8,128)(2,1)S(1)} collective-permute-done((bf16[80,1920]{1,0:T(8,128)(2,1)}, bf16[80,1920]{1,0:T(8,128)(2,1)S(1)}, u32[]{:S(2)}, u32[]{:S(2)}) %collective-permute-start.6) | collective-permute-done | bytes 307232 | tf_op jit(solution)/shard_map/ppermute | solution.py:844
  55.8 10.5 %collective-permute-done.2.refs_3_ = bf16[256,640]{1,0:T(8,128)(2,1)S(1)} collective-permute-done((bf16[256,640]{1,0:T(8,128)(2,1)}, bf16[256,640]{1,0:T(8,128)(2,1)S(1)}, u32[]{:S(2)}, u32[]{:S(2)}) %collective-permute-start.2) | collective-permute-done | bytes 327712 | tf_op jit(solution)/shard_map/ppermute | solution.py:832
  67.1 4.2 %first_norm.1 = (bf16[1024,640]{1,0:T(8,128)(2,1)}, bf16[1024,640]{1,0:T(8,128)(2,1)}, bf16[4,80,1920]{2,1,0:T(8,128)(2,1)}) custom-call(s32[6]{0:T(128)} %stack.31.refs_0_.place_ref, bf16[256,640]{1,0:T(8,128)(2,1)} %get-tuple-element.61.refs_1_, bf16[256,640]{1,0:T(8,128)(2,1)} %copy-done.6, bf16[256,640]{1,0:T(8,128)(2,1)} %copy-done.7, ...), custom_call_target="tpu_custom_call" | custom-call | bytes 5089280 | tf_op jit(solution)/shard_map/first_norm/pallas_call | solution.py:90
  76.0 8.5 %project.1 = (bf16[1024,1920]{1,0:T(8,128)(2,1)}, bf16[640,1920]{1,0:T(8,128)(2,1)}) custom-call(s32[6]{0:T(128)} %stack.31.refs_0_.place_ref, bf16[1024,640]{1,0:T(8,128)(2,1)} %get-tuple-element.66.normed_ref, f32[1,1920]{1,0:T(1,128)} %bitcast.14, f32[1024,128]{1,0:T(8,128)} %constant.36.clone.cos_ref, f32[1024,128]{1,0:T(8,128)} %constant.37.clone.sin_ref, ...), custom_call_target="tpu_custom_call" | custom-call | flops 2516582400 | bytes 7864320 | tf_op jit(solution)/shard_map/project/pallas_call | solution.py:354
  84.5 2.4 pick.3
  86.9 7.0 %collective-permute-start.10 = (bf16[256,640]{1,0:T(8,128)(2,1)}, bf16[256,640]{1,0:T(8,128)(2,1)S(1)}, u32[]{:S(2)}, u32[]{:S(2)}) collective-permute-start(bf16[256,640]{1,0:T(8,128)(2,1)} %get-tuple-element.71), channel_id=1, source_target_pairs={{0,1},{1,2},{3,0},{4,5},{5,6},{6,7},{8,9},{9,10},{11,8},{12,13},{1... | collective-permute-start | bytes 983048 | tf_op jit(solution)/shard_map/ppermute | solution.py:832
  93.9 1.9 collective-permute-start.11
  95.8 1.5 collective-permute-start.12
  97.3 16.7 %attend.1 = (bf16[1024,640]{1,0:T(8,128)(2,1)}, f32[1024,640]{1,0:T(8,128)}) custom-call(s32[6]{0:T(128)} %stack.31.refs_0_.place_ref, s32[3,4]{1,0:T(4,128)} %lens_ref.5, bf16[1024,1920]{1,0:T(8,128)(2,1)} %get-tuple-element.68.q_ref.k_ref.v_ref.refs_2_, bf16[1024,1920]{1,0:T(8,128)(2,1)} %get-tuple-element.68.q_ref.k_ref.v_ref.refs_2_, ...), custom_call_target="tpu_custom_call" | custom-call | flops 64424509440 | bytes 7864320 | tf_op jit(solution)/shard_map/attend/pallas_call | solution.py:442
  114.0 3.8 %collective-permute-done.11.refs_3_ = bf16[256,640]{1,0:T(8,128)(2,1)S(1)} collective-permute-done((bf16[256,640]{1,0:T(8,128)(2,1)}, bf16[256,640]{1,0:T(8,128)(2,1)S(1)}, u32[]{:S(2)}, u32[]{:S(2)}) %collective-permute-start.11) | collective-permute-done | bytes 327712 | tf_op jit(solution)/shard_map/ppermute | solution.py:832
  118.6 47.9 %feed.1 = (bf16[256,640]{1,0:T(8,128)(2,1)}, bf16[256,640]{1,0:T(8,128)(2,1)}, bf16[256,640]{1,0:T(8,128)(2,1)}, bf16[256,640]{1,0:T(8,128)(2,1)}, f32[1024,640]...) custom-call(s32[6]{0:T(128)} %stack.31.refs_0_.place_ref, ...), custom_call_target="tpu_custom_call" | custom-call | flops 22649241600 | bytes 39321600 | tf_op jit(solution)/shard_map/feed/pallas_call | solution.py:667
  167.4 5.9 %collective-permute-start.13 = (bf16[256,640]{1,0:T(8,128)(2,1)S(1)}, bf16[256,640]{1,0:T(8,128)(2,1)S(1)}, u32[]{:S(2)}, u32[]{:S(2)}) collective-permute-start(bf16[256,640]{1,0:T(8,128)(2,1)S(1)} %copy-done.41), channel_id=1, source_target_pairs={{0,1},{1,2},{2,3},{5,6},{6,7},{7,4},{8,9},{9,10},{10,11},{13,14},{... | collective-permute-start | bytes 983048 | tf_op jit(solution)/shard_map/ppermute | solution.py:837
  173.4 1.9 collective-permute-start.14
  175.3 1.9 collective-permute-start.15
  177.2 29.9 %attend_back.1 = (bf16[1024,640]{1,0:T(8,128)(2,1)}, bf16[1024,640]{1,0:T(8,128)(2,1)}, bf16[1024,640]{1,0:T(8,128)(2,1)}) custom-call(s32[6]{0:T(128)} %stack.31.refs_0_.place_ref, s32[3,4]{1,0:T(4,128)} %lens_ref.5, bf16[1024,1920]{1,0:T(8,128)(2,1)} %get-tuple-element.68.q_ref.k_ref.v_ref.refs_2_, ...), custom_call_target="tpu_custom_call" | custom-call | flops 128849018880 | bytes 13107200 | tf_op jit(solution)/shard_map/attend_back/pallas_call | solution.py:528
  208.1 2.4 put.2.refs_0_
  210.5 8.0 %project_grads.1 = (bf16[4,80,1920]{2,1,0:T(8,128)(2,1)}, bf16[4,80,1920]{2,1,0:T(8,128)(2,1)}, f32[8,640]{1,0:T(8,128)}) custom-call(s32[6]{0:T(128)} %stack.31.refs_0_.place_ref, bf16[1024,640]{1,0:T(8,128)(2,1)} %get-tuple-element.66.normed_ref, bf16[1024,640]{1,0:T(8,128)(2,1)} %get-tuple-element.80.q_ref, bf16[1024,640]{1,0:T(8,128)(2,1)} %get-tuple-element.81.k_ref, ...), custom_call_target="tpu_custom_call" | custom-call | flops 2516582400 | bytes 9175040 | tf_op jit(solution)/shard_map/project_grads/pallas_call | solution.py:736
  218.5 25.4 %reduce-scatter.3.cloned.1.call-done.refs_0_ = bf16[80,5760]{1,0:T(8,128)(2,1)} async-done(((bf16[640,5760]{1,0:T(8,128)(2,1)}), bf16[80,5760]{1,0:T(8,128)(2,1)}) %reduce-scatter.3.cloned.1.call-update) | async-done | bytes 921616 | tf_op jit(solution)/shard_map/reduce_scatter | solution.py:875
  243.9 2.3 by_owner.1
  246.2 9.3 %project_back.1 = (bf16[256,640]{1,0:T(8,128)(2,1)}, bf16[256,640]{1,0:T(8,128)(2,1)}, bf16[256,640]{1,0:T(8,128)(2,1)}, bf16[256,640]{1,0:T(8,128)(2,1)}, f32[8,640]{1,0:T(8,128)}) custom-call(s32[6]{0:T(128)} %stack.31.refs_0_.place_ref, bf16[1024,640]{1,0:T(8,128)(2,1)} %get-tuple-element.80.q_ref, bf16[1024,640]{1,0:T(8,128)(2,1)} %get-tuple-element.81.k_ref, ...), custom_call_target="tpu_custom_call" | custom-call | flops 2516582400 | bytes 10485760 | tf_op jit(solution)/shard_map/project_back/pallas_call | solution.py:775
  256.4 1.2 collective-permute-done.20.refs_4_
  258.7 3.0 pair_sums.1
  261.7 15.5 %collective-permute-start.21 = (bf16[96,1920]{1,0:T(8,128)(2,1)}, bf16[96,1920]{1,0:T(8,128)(2,1)S(1)}, u32[]{:S(2)}, u32[]{:S(2)}) collective-permute-start(bf16[96,1920]{1,0:T(8,128)(2,1)} %get-tuple-element.95), channel_id=1, source_target_pairs={{0,8},{4,12},{8,0},{12,4},{16,24},{20,28},{24,16},{28,20},{1,9},{5... | collective-permute-start | bytes 1105928 | tf_op jit(solution)/shard_map/ppermute | solution.py:844
  278.7 3.2 collective-permute-start.16
  281.8 1.9 collective-permute-start.17
  283.8 3.0 collective-permute-done.21.refs_2_
  286.7 1.9 collective-permute-start.18
  288.7 7.2 %collective-permute-done.22.refs_3_ = bf16[96,1920]{1,0:T(8,128)(2,1)S(1)} collective-permute-done((bf16[96,1920]{1,0:T(8,128)(2,1)}, bf16[96,1920]{1,0:T(8,128)(2,1)S(1)}, u32[]{:S(2)}, u32[]{:S(2)}) %collective-permute-start.22) | collective-permute-done | bytes 368672 | tf_op jit(solution)/shard_map/ppermute | solution.py:844
  296.7 3.3 plane_sums.1
  301.2 2.9 collective-permute-start.26
  304.1 4.8 %collective-permute-done.18.refs_4_ = bf16[256,640]{1,0:T(8,128)(2,1)S(1)} collective-permute-done((bf16[256,640]{1,0:T(8,128)(2,1)S(1)}, bf16[256,640]{1,0:T(8,128)(2,1)S(1)}, u32[]{:S(2)}, u32[]{:S(2)}) %collective-permute-start.18) | collective-permute-done | bytes 327712 | tf_op jit(solution)/shard_map/ppermute | solution.py:837
  309.6 2.7 put.3
  312.4 3.0 collective-permute-done.25.refs_3_
  316.1 1.9 last_sums.1
  320.9 1.7 total_of.1
  (143 shorter events, 22.2 us)
Async XLA Ops:
  7.2 9.7 %copy-start = (s32[3,1]{0,1:T(1,128)S(1)}, s32[3,1]{0,1:T(1,128)}, u32[]{:S(2)}) copy-start(s32[3,1]{0,1:T(1,128)} %param.22) | copy-start | bytes 40
  7.2 34.9 %copy-start.29 = (f32[640]{0:T(1024)S(1)}, f32[640]{0:T(1024)}, u32[]{:S(2)}) copy-start(f32[640]{0:T(1024)} %param.24) | copy-start | bytes 7684
  7.2 35.5 %copy-start.30 = (f32[640]{0:T(1024)S(1)}, f32[640]{0:T(1024)}, u32[]{:S(2)}) copy-start(f32[640]{0:T(1024)} %param.25) | copy-start | bytes 7684
  7.2 110.5 %all-gather.3.cloned.1.call-start = ((), (), s32[]{:S(2)}) async-start(), calls=%async_computation.4 | async-start | bytes 8110080 | tf_op jit(solution)/shard_map/all_gather | solution.py:855
  8.9 235.0 %reduce-scatter.3.cloned.1.call-start = ((), (), s32[]{:S(2)}) async-start(), calls=%async_computation.2 | async-start | bytes 8294400 | tf_op jit(solution)/shard_map/reduce_scatter | solution.py:875
  9.0 13.8 %collective-permute-start.4 = (bf16[3,80,160]{2,1,0:T(8,128)(2,1)}, bf16[3,80,160]{2,1,0:T(8,128)(2,1)S(1)}, u32[]{:S(2)}, u32[]{:S(2)}) collective-permute-start(bf16[3,80,160]{2,1,0:T(8,128)(2,1)} %refs_1_.5), channel_id=1, source_target_pairs={{0,2},{1,3},{2,0},{3,1},{4,6},{5,7},{6,4},{7,5},{8,10},{9,11},{10,... | collective-permute-start | bytes 230408 | tf_op jit(solution)/shard_map/ppermute | solution.py:841
  13.1 9.7 %collective-permute-start = (bf16[3,80,160]{2,1,0:T(8,128)(2,1)}, bf16[3,80,160]{2,1,0:T(8,128)(2,1)S(1)}, u32[]{:S(2)}, u32[]{:S(2)}) collective-permute-start(bf16[3,80,160]{2,1,0:T(8,128)(2,1)} %refs_1_.5), channel_id=1, source_target_pairs={{0,1},{1,2},{2,3},{3,0},{4,5},{5,6},{6,7},{7,4},{8,9},{9,10},{10,1... | collective-permute-start | bytes 230408 | tf_op jit(solution)/shard_map/ppermute | solution.py:841
  14.7 8.8 %collective-permute-start.5 = (bf16[3,80,160]{2,1,0:T(8,128)(2,1)}, bf16[3,80,160]{2,1,0:T(8,128)(2,1)S(1)}, u32[]{:S(2)}, u32[]{:S(2)}) collective-permute-start(bf16[3,80,160]{2,1,0:T(8,128)(2,1)} %refs_1_.5), channel_id=1, source_target_pairs={{0,3},{1,0},{2,1},{3,2},{4,7},{5,4},{6,5},{7,6},{8,11},{9,8},{10,9... | collective-permute-start | bytes 230408 | tf_op jit(solution)/shard_map/ppermute | solution.py:841
  26.1 14.9 %collective-permute-start.8 = (bf16[80,1920]{1,0:T(8,128)(2,1)}, bf16[80,1920]{1,0:T(8,128)(2,1)S(1)}, u32[]{:S(2)}, u32[]{:S(2)}) collective-permute-start(bf16[80,1920]{1,0:T(8,128)(2,1)} %arrange.1.refs_7_), channel_id=1, source_target_pairs={{0,24},{4,28},{8,16},{12,20},{16,8},{20,12},{24,0},{28,4},{1,25},{... | collective-permute-start | bytes 921608 | tf_op jit(solution)/shard_map/ppermute | solution.py:844
  31.3 40.1 %copy-start.31 = (f32[640]{0:T(1024)S(1)}, f32[640]{0:T(1024)}, u32[]{:S(2)}) copy-start(f32[640]{0:T(1024)} %param.26) | copy-start | bytes 7684
  31.3 40.7 %copy-start.32 = (f32[640]{0:T(1024)S(1)}, f32[640]{0:T(1024)}, u32[]{:S(2)}) copy-start(f32[640]{0:T(1024)} %param.27) | copy-start | bytes 7684
  31.3 41.2 %copy-start.33 = (f32[640]{0:T(1024)S(1)}, f32[640]{0:T(1024)}, u32[]{:S(2)}) copy-start(f32[640]{0:T(1024)} %param.31) | copy-start | bytes 7684
  31.3 41.8 %copy-start.34 = (f32[640]{0:T(1024)S(1)}, f32[640]{0:T(1024)}, u32[]{:S(2)}) copy-start(f32[640]{0:T(1024)} %param.35) | copy-start | bytes 7684
  31.3 42.4 %copy-start.27 = (f32[3,640]{1,0:T(4,128)S(1)}, f32[3,640]{1,0:T(4,128)}, u32[]{:S(2)}) copy-start(f32[3,640]{1,0:T(4,128)} %param.29) | copy-start | bytes 23044
  31.3 43.0 %copy-start.25 = (f32[2560]{0:T(1024)S(1)}, f32[2560]{0:T(1024)}, u32[]{:S(2)}) copy-start(f32[2560]{0:T(1024)} %param.33) | copy-start | bytes 30724
  31.3 24.4 %collective-permute-start.1 = (bf16[256,640]{1,0:T(8,128)(2,1)}, bf16[256,640]{1,0:T(8,128)(2,1)S(1)}, u32[]{:S(2)}, u32[]{:S(2)}) collective-permute-start(bf16[256,640]{1,0:T(8,128)(2,1)} %get-tuple-element.62), channel_id=1, source_target_pairs={{0,1},{1,2},{3,0},{4,5},{5,6},{6,7},{8,9},{9,10},{11,8},{12,13},{1... | collective-permute-start | bytes 983048 | tf_op jit(solution)/shard_map/ppermute | solution.py:832
  35.6 30.6 %collective-permute-start.2 = (bf16[256,640]{1,0:T(8,128)(2,1)}, bf16[256,640]{1,0:T(8,128)(2,1)S(1)}, u32[]{:S(2)}, u32[]{:S(2)}) collective-permute-start(bf16[256,640]{1,0:T(8,128)(2,1)} %get-tuple-element.63), channel_id=1, source_target_pairs={{0,2},{2,0},{3,1},{4,6},{5,7},{7,5},{8,10},{10,8},{11,9},{12,14},{... | collective-permute-start | bytes 983048 | tf_op jit(solution)/shard_map/ppermute | solution.py:832
  39.4 26.9 %collective-permute-start.3 = (bf16[256,640]{1,0:T(8,128)(2,1)}, bf16[256,640]{1,0:T(8,128)(2,1)S(1)}, u32[]{:S(2)}, u32[]{:S(2)}) collective-permute-start(bf16[256,640]{1,0:T(8,128)(2,1)} %get-tuple-element.64), channel_id=1, source_target_pairs={{1,0},{2,1},{3,2},{4,7},{6,5},{7,6},{9,8},{10,9},{11,10},{12,15},{... | collective-permute-start | bytes 983048 | tf_op jit(solution)/shard_map/ppermute | solution.py:832
  40.7 11.5 %collective-permute-start.7 = (bf16[80,1920]{1,0:T(8,128)(2,1)}, bf16[80,1920]{1,0:T(8,128)(2,1)S(1)}, u32[]{:S(2)}, u32[]{:S(2)}) collective-permute-start(bf16[80,1920]{1,0:T(8,128)(2,1)} %arrange.1.refs_7_), channel_id=1, source_target_pairs={{0,16},{4,20},{8,24},{12,28},{16,0},{20,4},{24,8},{28,12},{1,17},{... | collective-permute-start | bytes 921608 | tf_op jit(solution)/shard_map/ppermute | solution.py:844
  41.0 25.3 %copy-start.15 = (bf16[80,1920]{1,0:T(8,128)(2,1)}, bf16[80,1920]{1,0:T(8,128)(2,1)S(1)}, u32[]{:S(2)}) copy-start(bf16[80,1920]{1,0:T(8,128)(2,1)S(1)} %collective-permute-done.8.refs_10_) | copy-start | bytes 921604
  41.0 14.7 %collective-permute-start.6 = (bf16[80,1920]{1,0:T(8,128)(2,1)}, bf16[80,1920]{1,0:T(8,128)(2,1)S(1)}, u32[]{:S(2)}, u32[]{:S(2)}) collective-permute-start(bf16[80,1920]{1,0:T(8,128)(2,1)} %arrange.1.refs_7_), channel_id=1, source_target_pairs={{0,8},{4,12},{8,0},{12,4},{16,24},{20,28},{24,16},{28,20},{1,9},{5... | collective-permute-start | bytes 921608 | tf_op jit(solution)/shard_map/ppermute | solution.py:844
  52.1 14.1 %copy-start.16 = (bf16[80,1920]{1,0:T(8,128)(2,1)}, bf16[80,1920]{1,0:T(8,128)(2,1)S(1)}, u32[]{:S(2)}) copy-start(bf16[80,1920]{1,0:T(8,128)(2,1)S(1)} %collective-permute-done.7.refs_9_) | copy-start | bytes 921604
  55.7 10.5 %copy-start.17 = (bf16[80,1920]{1,0:T(8,128)(2,1)}, bf16[80,1920]{1,0:T(8,128)(2,1)S(1)}, u32[]{:S(2)}) copy-start(bf16[80,1920]{1,0:T(8,128)(2,1)S(1)} %collective-permute-done.6.refs_8_) | copy-start | bytes 921604
  55.8 10.5 %copy-start.6 = (bf16[256,640]{1,0:T(8,128)(2,1)}, bf16[256,640]{1,0:T(8,128)(2,1)S(1)}, u32[]{:S(2)}) copy-start(bf16[256,640]{1,0:T(8,128)(2,1)S(1)} %collective-permute-done.1.refs_2_) | copy-start | bytes 983044
  71.3 3.6 %collective-permute-start.9 = (bf16[4,80,1920]{2,1,0:T(8,128)(2,1)}, bf16[4,80,1920]{2,1,0:T(8,128)(2,1)S(1)}, u32[]{:S(2)}, u32[]{:S(2)}) collective-permute-start(bf16[4,80,1920]{2,1,0:T(8,128)(2,1)} %get-tuple-element.67.refs_0_), channel_id=1, source_target_pairs={{0,4},{4,0},{8,12},{12,8},{16,20},{20,16},{24,28},{28,24},{1,5},{5... | collective-permute-start | bytes 3686408 | tf_op jit(solution)/shard_map/ppermute | solution.py:844
  86.9 27.1 %collective-permute-start.10 = (bf16[256,640]{1,0:T(8,128)(2,1)}, bf16[256,640]{1,0:T(8,128)(2,1)S(1)}, u32[]{:S(2)}, u32[]{:S(2)}) collective-permute-start(bf16[256,640]{1,0:T(8,128)(2,1)} %get-tuple-element.71), channel_id=1, source_target_pairs={{0,1},{1,2},{3,0},{4,5},{5,6},{6,7},{8,9},{9,10},{11,8},{12,13},{1... | collective-permute-start | bytes 983048 | tf_op jit(solution)/shard_map/ppermute | solution.py:832
  93.9 23.9 %collective-permute-start.11 = (bf16[256,640]{1,0:T(8,128)(2,1)}, bf16[256,640]{1,0:T(8,128)(2,1)S(1)}, u32[]{:S(2)}, u32[]{:S(2)}) collective-permute-start(bf16[256,640]{1,0:T(8,128)(2,1)} %get-tuple-element.72), channel_id=1, source_target_pairs={{0,2},{2,0},{3,1},{4,6},{5,7},{7,5},{8,10},{10,8},{11,9},{12,14},{... | collective-permute-start | bytes 983048 | tf_op jit(solution)/shard_map/ppermute | solution.py:832
  95.8 21.9 %collective-permute-start.12 = (bf16[256,640]{1,0:T(8,128)(2,1)}, bf16[256,640]{1,0:T(8,128)(2,1)S(1)}, u32[]{:S(2)}, u32[]{:S(2)}) collective-permute-start(bf16[256,640]{1,0:T(8,128)(2,1)} %get-tuple-element.73), channel_id=1, source_target_pairs={{1,0},{2,1},{3,2},{4,7},{6,5},{7,6},{9,8},{10,9},{11,10},{12,15},{... | collective-permute-start | bytes 983048 | tf_op jit(solution)/shard_map/ppermute | solution.py:832
  166.5 154.5 %reduce-scatter.5.cloned.1.call-start = ((), (), s32[]{:S(2)}) async-start(), calls=%async_computation.3 | async-start | bytes 1228800 | tf_op jit(solution)/shard_map/reduce_scatter | solution.py:877
  167.4 39.7 %collective-permute-start.13 = (bf16[256,640]{1,0:T(8,128)(2,1)S(1)}, bf16[256,640]{1,0:T(8,128)(2,1)S(1)}, u32[]{:S(2)}, u32[]{:S(2)}) collective-permute-start(bf16[256,640]{1,0:T(8,128)(2,1)S(1)} %copy-done.41), channel_id=1, source_target_pairs={{0,1},{1,2},{2,3},{5,6},{6,7},{7,4},{8,9},{9,10},{10,11},{13,14},{... | collective-permute-start | bytes 983048 | tf_op jit(solution)/shard_map/ppermute | solution.py:837
  173.4 33.8 %collective-permute-start.14 = (bf16[256,640]{1,0:T(8,128)(2,1)S(1)}, bf16[256,640]{1,0:T(8,128)(2,1)S(1)}, u32[]{:S(2)}, u32[]{:S(2)}) collective-permute-start(bf16[256,640]{1,0:T(8,128)(2,1)S(1)} %copy-done.40), channel_id=1, source_target_pairs={{0,2},{1,3},{2,0},{5,7},{6,4},{7,5},{8,10},{9,11},{10,8},{13,15},{... | collective-permute-start | bytes 983048 | tf_op jit(solution)/shard_map/ppermute | solution.py:837
  175.3 31.9 %collective-permute-start.15 = (bf16[256,640]{1,0:T(8,128)(2,1)S(1)}, bf16[256,640]{1,0:T(8,128)(2,1)S(1)}, u32[]{:S(2)}, u32[]{:S(2)}) collective-permute-start(bf16[256,640]{1,0:T(8,128)(2,1)S(1)} %copy-done.39), channel_id=1, source_target_pairs={{0,3},{1,0},{2,1},{5,4},{6,5},{7,6},{8,11},{9,8},{10,9},{13,12},{1... | collective-permute-start | bytes 983048 | tf_op jit(solution)/shard_map/ppermute | solution.py:837
  218.5 39.2 %collective-permute-start.19 = (bf16[4,80,1920]{2,1,0:T(8,128)(2,1)}, bf16[4,80,1920]{2,1,0:T(8,128)(2,1)S(1)}, u32[]{:S(2)}, u32[]{:S(2)}) collective-permute-start(bf16[4,80,1920]{2,1,0:T(8,128)(2,1)} %get-tuple-element.90), channel_id=1, source_target_pairs={{0,4},{4,0},{8,12},{12,8},{16,20},{20,16},{24,28},{28,24},{1,5},{5... | collective-permute-start | bytes 3686408 | tf_op jit(solution)/shard_map/ppermute | solution.py:844
  246.2 10.0 %copy-start.26 = (f32[16,640]{1,0:T(8,128)S(1)}, f32[16,640]{1,0:T(8,128)}, u32[]{:S(2)}) copy-start(f32[16,640]{1,0:T(8,128)} %get-tuple-element.91) | copy-start | bytes 122884
  246.2 10.0 %copy-start.28 = (f32[8,640]{1,0:T(8,128)S(1)}, f32[8,640]{1,0:T(8,128)}, u32[]{:S(2)}) copy-start(f32[8,640]{1,0:T(8,128)} %get-tuple-element.92) | copy-start | bytes 61444
  256.3 22.4 %copy-start.38 = (bf16[256,640]{1,0:T(8,128)(2,1)S(1)}, bf16[256,640]{1,0:T(8,128)(2,1)}, u32[]{:S(2)}) copy-start(bf16[256,640]{1,0:T(8,128)(2,1)} %get-tuple-element.86) | copy-start | bytes 983044
  256.3 25.6 %copy-start.37 = (bf16[256,640]{1,0:T(8,128)(2,1)S(1)}, bf16[256,640]{1,0:T(8,128)(2,1)}, u32[]{:S(2)}) copy-start(bf16[256,640]{1,0:T(8,128)(2,1)} %get-tuple-element.87) | copy-start | bytes 983044
  256.3 30.5 %copy-start.36 = (bf16[256,640]{1,0:T(8,128)(2,1)S(1)}, bf16[256,640]{1,0:T(8,128)(2,1)}, u32[]{:S(2)}) copy-start(bf16[256,640]{1,0:T(8,128)(2,1)} %get-tuple-element.88) | copy-start | bytes 983044
  256.3 1.3 collective-permute-start.20
  261.7 25.1 %collective-permute-start.21 = (bf16[96,1920]{1,0:T(8,128)(2,1)}, bf16[96,1920]{1,0:T(8,128)(2,1)S(1)}, u32[]{:S(2)}, u32[]{:S(2)}) collective-permute-start(bf16[96,1920]{1,0:T(8,128)(2,1)} %get-tuple-element.95), channel_id=1, source_target_pairs={{0,8},{4,12},{8,0},{12,4},{16,24},{20,28},{24,16},{28,20},{1,9},{5... | collective-permute-start | bytes 1105928 | tf_op jit(solution)/shard_map/ppermute | solution.py:844
  277.2 18.7 %collective-permute-start.22 = (bf16[96,1920]{1,0:T(8,128)(2,1)}, bf16[96,1920]{1,0:T(8,128)(2,1)S(1)}, u32[]{:S(2)}, u32[]{:S(2)}) collective-permute-start(bf16[96,1920]{1,0:T(8,128)(2,1)} %get-tuple-element.96), channel_id=1, source_target_pairs={{0,16},{4,20},{8,24},{12,28},{16,0},{20,4},{24,8},{28,12},{1,17},{... | collective-permute-start | bytes 1105928 | tf_op jit(solution)/shard_map/ppermute | solution.py:844
  277.7 18.2 %collective-permute-start.23 = (bf16[96,1920]{1,0:T(8,128)(2,1)}, bf16[96,1920]{1,0:T(8,128)(2,1)S(1)}, u32[]{:S(2)}, u32[]{:S(2)}) collective-permute-start(bf16[96,1920]{1,0:T(8,128)(2,1)} %get-tuple-element.97), channel_id=1, source_target_pairs={{0,24},{4,28},{8,16},{12,20},{16,8},{20,12},{24,0},{28,4},{1,25},{... | collective-permute-start | bytes 1105928 | tf_op jit(solution)/shard_map/ppermute | solution.py:844
  278.7 22.5 %collective-permute-start.16 = (bf16[256,640]{1,0:T(8,128)(2,1)S(1)}, bf16[256,640]{1,0:T(8,128)(2,1)S(1)}, u32[]{:S(2)}, u32[]{:S(2)}) collective-permute-start(bf16[256,640]{1,0:T(8,128)(2,1)S(1)} %copy-done.38), channel_id=1, source_target_pairs={{0,1},{1,2},{2,3},{5,6},{6,7},{7,4},{8,9},{9,10},{10,11},{13,14},{... | collective-permute-start | bytes 983048 | tf_op jit(solution)/shard_map/ppermute | solution.py:837
  281.8 22.2 %collective-permute-start.17 = (bf16[256,640]{1,0:T(8,128)(2,1)S(1)}, bf16[256,640]{1,0:T(8,128)(2,1)S(1)}, u32[]{:S(2)}, u32[]{:S(2)}) collective-permute-start(bf16[256,640]{1,0:T(8,128)(2,1)S(1)} %copy-done.37), channel_id=1, source_target_pairs={{0,2},{1,3},{2,0},{5,7},{6,4},{7,5},{8,10},{9,11},{10,8},{13,15},{... | collective-permute-start | bytes 983048 | tf_op jit(solution)/shard_map/ppermute | solution.py:837
  286.7 22.2 %collective-permute-start.18 = (bf16[256,640]{1,0:T(8,128)(2,1)S(1)}, bf16[256,640]{1,0:T(8,128)(2,1)S(1)}, u32[]{:S(2)}, u32[]{:S(2)}) collective-permute-start(bf16[256,640]{1,0:T(8,128)(2,1)S(1)} %copy-done.36), channel_id=1, source_target_pairs={{0,3},{1,0},{2,1},{5,4},{6,5},{7,6},{8,11},{9,8},{10,9},{13,12},{1... | collective-permute-start | bytes 983048 | tf_op jit(solution)/shard_map/ppermute | solution.py:837
  300.0 12.4 %collective-permute-start.24 = (bf16[144,480]{1,0:T(8,128)(2,1)}, bf16[144,480]{1,0:T(8,128)(2,1)S(1)}, u32[]{:S(2)}, u32[]{:S(2)}) collective-permute-start(bf16[144,480]{1,0:T(8,128)(2,1)} %get-tuple-element.99), channel_id=1, source_target_pairs={{0,1},{1,2},{2,3},{3,0},{4,5},{5,6},{6,7},{7,4},{8,9},{9,10},{10,1... | collective-permute-start | bytes 414728 | tf_op jit(solution)/shard_map/ppermute | solution.py:841
  301.0 14.4 %collective-permute-start.25 = (bf16[144,480]{1,0:T(8,128)(2,1)}, bf16[144,480]{1,0:T(8,128)(2,1)S(1)}, u32[]{:S(2)}, u32[]{:S(2)}) collective-permute-start(bf16[144,480]{1,0:T(8,128)(2,1)} %get-tuple-element.100), channel_id=1, source_target_pairs={{0,2},{1,3},{2,0},{3,1},{4,6},{5,7},{6,4},{7,5},{8,10},{9,11},{10,... | collective-permute-start | bytes 414728 | tf_op jit(solution)/shard_map/ppermute | solution.py:841
  301.2 14.2 %collective-permute-start.26 = (bf16[144,480]{1,0:T(8,128)(2,1)}, bf16[144,480]{1,0:T(8,128)(2,1)S(1)}, u32[]{:S(2)}, u32[]{:S(2)}) collective-permute-start(bf16[144,480]{1,0:T(8,128)(2,1)} %get-tuple-element.101), channel_id=1, source_target_pairs={{0,3},{1,0},{2,1},{3,2},{4,7},{5,4},{6,5},{7,6},{8,11},{9,8},{10,9... | collective-permute-start | bytes 414728 | tf_op jit(solution)/shard_map/ppermute | solution.py:841
  (27 other events, 60.7 us)
Sparse Core Ops, SparseCore 0:
  11.4 95.6 all-gather.2
  166.6 77.2 reduce-scatter.2
  246.4 38.8 reduce-scatter.4
